TPU v7x, 256 devices: a whole 4x4x8 slice. The times are simulated.
256 devices in a mesh: seq: 64 (over y_lo, x, z), mp: 4 (over y_hi, core).
Axes of the slice: x: 4, y: 4 (y_hi: 2, y_lo: 2; y = y_hi * 2 + y_lo), z: 8, core: 2. Of those that a mesh axis runs over, the one named last changes fastest.
Arguments:
- projected: bfloat16 [3, 4096, 16384], P(None, 'mp', 'seq'), may hold values from -6 to 6
- short_taps: float32 [3, 3, 4096], P(None, None, 'mp'), may hold values from -3.5 to 3.5
- long_filter: bfloat16 [4096, 16384], P('mp', 'seq'), may hold values from -0.046875 to 0.046875
- skip_gain: float32 [4096], P('mp'), may hold values from -4 to 4
- w_out: bfloat16 [4096, 4096], P(None, 'mp'), may hold values from -0.09375 to 0.09375
Outputs:
- mixed: bfloat16 [16384, 4096], P('seq', 'mp')
All inputs are finite; a program needn't handle non-finite values.
Results may differ from a plain program's by a relative error of at most 0.0081.
Values may be sent and summed in bfloat16 or wider, within the bound.
No kernel may reach another device: no remote copies, remote signals or barrier semaphores. Data moves between devices by JAX's collectives and lax.ppermute only.
A program may use at most 128 MiB of HBM per device.

v0:
```python
import jax
import jax.numpy as jnp
import ml_dtypes
import numpy as np
from jax import lax
from jax.experimental import pallas as pl
from jax.experimental.pallas import tpu as pltpu
from jax.sharding import PartitionSpec as P

N1 = 128
N2 = 128


def split(table):
    high = table.astype(ml_dtypes.bfloat16)
    low = (table - high.astype(np.float64)).astype(ml_dtypes.bfloat16)
    return high, low


def dft_tables(rows):
    order = np.concatenate([np.arange(0, N1, 2), np.arange(1, N1, 2)])
    k1 = np.arange(N1)
    first = 2.0 * np.pi * np.outer(k1 + 0.25, order) / N1
    stage1 = np.concatenate([np.cos(first), -np.sin(first)], axis=0)
    s1_hi, s1_lo = split(stage1)
    stage1 = np.concatenate([s1_hi, s1_lo], axis=1)
    turn = 2.0 * np.pi * np.outer(k1 + 0.25, np.arange(N2)) / (N1 * N2)
    turns = np.stack([np.cos(turn), np.sin(turn)]).astype(np.float32)
    second = 2.0 * np.pi * np.outer(np.arange(N2), np.arange(N2)) / N2
    cos, sin = np.cos(second), np.sin(second)
    forward2 = np.stack(split(np.block([[cos, -sin], [sin, cos]])))
    inverse2 = np.stack(split(np.block([[cos, sin], [-sin, cos]])))
    last = np.concatenate([np.cos(first.T), -np.sin(first.T)], axis=1) / (N1 * N2)
    inverse1 = np.concatenate(split(last), axis=0)
    return stage1, turns, forward2, inverse2, inverse1


def dot(a, b):
    return jnp.dot(a, b, preferred_element_type=jnp.float32)


def halves(value):
    high = value.astype(jnp.bfloat16)
    low = (value - high.astype(jnp.float32)).astype(jnp.bfloat16)
    return high, low


def wide_dot(value, table):
    high, low = halves(value)
    return dot(high, table[0]) + (dot(high, table[1]) + dot(low, table[0]))


def load_tile(flat, channel, parts, per_dev):
    picked = [
        half[pl.ds(channel, parts, stride=per_dev), :] for half in flat
    ]
    return jnp.concatenate(picked, axis=0)


def unpack(source, flat, parts, per_dev):
    for half in range(2):
        flat[half][...] = (
            source[:, :, half * N2 : (half + 1) * N2]
            .astype(jnp.float32)
            .reshape(parts * per_dev, N2)
        )


def spectrum_of(tiles, stage1, turns, forward2):
    pair = jnp.concatenate([tile.astype(jnp.bfloat16) for tile in tiles], axis=1)
    both = dot(stage1[...], jnp.concatenate([pair, pair], axis=0))
    cos, sin = turns[0], turns[1]
    result = []
    for place in range(len(tiles)):
        re = both[:N1, place * N2 : (place + 1) * N2]
        im = both[N1:, place * N2 : (place + 1) * N2]
        turned = jnp.concatenate([re * cos + im * sin, im * cos - re * sin], axis=1)
        result.append(wide_dot(turned, (forward2[0], forward2[1])))
    return result


def filter_kernel(received, stage1, turns, forward2, spectrum, even, odd):
    parts, per_dev, _ = received.shape
    flat = (even, odd)
    unpack(received, flat, parts, per_dev)
    for first in range(0, per_dev, 2):
        tiles = [load_tile(flat, first + place, parts, per_dev) for place in range(2)]
        for place, result in enumerate(spectrum_of(tiles, stage1, turns, forward2)):
            spectrum[first + place] = result


def conv_kernel(
    received, spectrum, skip, stage1, turns, forward2, inverse2, inverse1, response, even, odd
):
    parts, per_dev, _ = received.shape
    flat = (even, odd)
    unpack(received, flat, parts, per_dev)
    cos, sin = turns[0], turns[1]
    for first in range(0, per_dev, 2):
        tiles = [load_tile(flat, first + place, parts, per_dev) for place in range(2)]
        spectra = spectrum_of(tiles, stage1, turns, forward2)
        turned_back = []
        for place in range(2):
            sig_re, sig_im = spectra[place][:, :N2], spectra[place][:, N2:]
            ker = spectrum[first + place]
            ker_re, ker_im = ker[:, :N2], ker[:, N2:]
            prod = jnp.concatenate(
                [sig_re * ker_re - sig_im * ker_im, sig_re * ker_im + sig_im * ker_re], axis=1
            )
            back = wide_dot(prod, (inverse2[0], inverse2[1]))
            re, im = back[:, :N2], back[:, N2:]
            turned_back.append(
                jnp.concatenate([re * cos - im * sin, re * sin + im * cos], axis=0)
            )
        high, low = halves(jnp.concatenate(turned_back, axis=1))
        most = dot(inverse1[...], high)
        restored = most[:N1] + (most[N1:] + dot(inverse1[:N1, :], low))
        for place in range(2):
            out = restored[:, place * N2 : (place + 1) * N2] + skip[first + place] * tiles[place]
            for half in range(2):
                flat[half][pl.ds(first + place, parts, stride=per_dev), :] = out[
                    half * parts : (half + 1) * parts
                ]
    for half in range(2):
        response[:, :, half * N2 : (half + 1) * N2] = (
            flat[half][...].reshape(parts, per_dev, N2).astype(jnp.bfloat16)
        )


def call(kernel, out_shape, args, specs, scratch, flops, moved):
    return pl.pallas_call(
        kernel,
        out_shape=out_shape,
        in_specs=specs,
        out_specs=pl.BlockSpec(memory_space=pltpu.VMEM),
        scratch_shapes=scratch,
        compiler_params=pltpu.CompilerParams(vmem_limit_bytes=32 * 2**20),
        cost_estimate=pl.CostEstimate(flops=flops, bytes_accessed=moved, transcendentals=0),
    )(*args)


def whole():
    return pl.BlockSpec(memory_space=pltpu.VMEM)


def per_device(projected, short_taps, long_filter, skip_gain, w_out):
    tok_len = projected.shape[2]
    quarter = projected.shape[1]
    seq_parts = lax.axis_size("seq")
    per_dev = quarter // seq_parts
    chunks = (seq_parts, per_dev, tok_len)
    stage1, turns, forward2, inverse2, inverse1 = [jnp.asarray(t) for t in dft_tables(seq_parts)]

    filter_in = lax.all_to_all(long_filter.reshape(chunks), "seq", split_axis=0, concat_axis=0, tiled=True)

    rim = projected[:, :, tok_len - 2 :]
    before = lax.ppermute(rim, "seq", [(s, s + 1) for s in range(seq_parts - 1)])
    joined = jnp.concatenate([before, projected], axis=2).astype(jnp.float32)
    features = short_taps[:, 0, :, None] * joined[:, :, 2:]
    features = features + short_taps[:, 1, :, None] * joined[:, :, 1 : tok_len + 1]
    features = (features + short_taps[:, 2, :, None] * joined[:, :, 0:tok_len]).astype(jnp.bfloat16)
    gated = (features[1].astype(jnp.float32) * features[2].astype(jnp.float32)).astype(jnp.bfloat16)
    signal_in = lax.all_to_all(gated.reshape(chunks), "seq", split_axis=0, concat_axis=0, tiled=True)

    scratch = [pltpu.VMEM((seq_parts * per_dev, N2), jnp.float32) for _ in range(2)]
    spectrum = call(
        filter_kernel,
        jax.ShapeDtypeStruct((per_dev, N1, 2 * N2), jnp.float32),
        (filter_in, stage1, turns, forward2),
        [whole()] * 4,
        scratch,
        2_000_000_000,
        4_000_000,
    )
    own_skip = lax.dynamic_slice_in_dim(skip_gain, lax.axis_index("seq") * per_dev, per_dev, 0)
    response = call(
        conv_kernel,
        jax.ShapeDtypeStruct(chunks, jnp.bfloat16),
        (signal_in, spectrum, own_skip, stage1, turns, forward2, inverse2, inverse1),
        [whole(), whole(), pl.BlockSpec(memory_space=pltpu.SMEM)] + [whole()] * 5,
        scratch,
        4_000_000_000,
        4_000_000,
    )
    returned = lax.all_to_all(response, "seq", split_axis=0, concat_axis=0, tiled=True)
    product = (
        features[0].astype(jnp.float32) * returned.reshape(quarter, tok_len).astype(jnp.float32)
    ).astype(jnp.bfloat16)

    me = lax.axis_index("mp")
    far = lax.ppermute(product, "mp", [(m, m ^ 2) for m in range(4)])
    near = lax.ppermute(product, "mp", [(m, m ^ 1) for m in range(4)])

    def part(value, flip):
        rows = lax.dynamic_slice_in_dim(w_out, (me ^ flip) * quarter, quarter, 0)
        return lax.dot_general(
            value, rows, (((0,), (0,)), ((), ())), preferred_element_type=jnp.float32
        )

    total = part(product, 0) + part(near, 1)
    last = lax.ppermute(far, "mp", [(m, m ^ 1) for m in range(4)])
    total = total + part(far, 2) + part(last, 3)
    return total.astype(jnp.bfloat16)


def solution(mesh):
    return jax.shard_map(
        per_device,
        mesh=mesh,
        in_specs=(
            P(None, "mp", "seq"),
            P(None, None, "mp"),
            P("mp", "seq"),
            P("mp"),
            P(None, "mp"),
        ),
        out_specs=P("seq", "mp"),
        check_vma=False,
    )
```

profile of v0, /device:TPU:1, one launch (start us, length us, event | category | flops | bytes accessed | tf_op | source)
XLA Modules:
  0.0 108.2 jit_solution(14395619250592755313)
XLA Ops:
  0.0 0.0 copy-start.7
  0.0 0.0 copy-start.8
  0.0 1.5 %slice.31 = bf16[3,1024,2]{2,1,0:T(8,128)(2,1)S(1)} slice(bf16[3,1024,256]{2,1,0:T(8,128)(2,1)} %param.10), slice={[0:3], [0:1024], [254:256]} | slice | bytes 24576 | tf_op jit(solution)/shard_map/slice | solution.py:156
  1.5 0.4 copy.16
  1.9 4.4 %collective-permute-start = (bf16[3,1024,2]{1,0,2:T(4,128)(2,1)S(1)}, bf16[3,1024,2]{1,0,2:T(4,128)(2,1)S(1)}, u32[]{:S(2)}, u32[]{:S(2)}) collective-permute-start(bf16[3,1024,2]{1,0,2:T(4,128)(2,1)S(1)} %copy.16), channel_id=1, source_target_pairs={{0,4},{4,8},{8,12},{12,16},{16,20},{20,24},{24,28},{28,32},{32,36}... | collective-permute-start | bytes 36872 | tf_op jit(solution)/shard_map/ppermute | solution.py:157
  6.3 11.8 %all-to-all-start.1 = ((bf16[64,16,256]{2,1,0:T(8,128)(2,1)}), bf16[64,16,256]{2,1,0:T(8,128)(2,1)S(1)}, u32[]{:S(2)}, u32[]{:S(2)}) async-start(bf16[64,16,256]{2,1,0:T(8,128)(2,1)} %bitcast.22), calls=%async_computation.1 | async-start | bytes 1048576 | tf_op jit(solution)/shard_map/all_to_all | solution.py:154
  18.1 0.0 copy-done.8
  18.2 0.0 collective-permute-done
  18.2 0.4 copy.12
  18.6 0.0 copy-done.7
  18.6 1.0 maximum_convert_fusion
  19.6 0.0 copy-start
  19.6 0.0 copy-start.2
  19.6 0.0 copy-start.3
  19.6 3.2 %fusion.1 = bf16[3,1024,256]{2,1,0:T(8,128)(2,1)S(1)} fusion(f32[3,1024,258]{2,1,0:T(8,128)S(1)} %maximum_convert_fusion, f32[3,1024]{1,0:T(4,128)S(1)} %get-tuple-element.8, f32[3,1024]{1,0:T(4,128)S(1)} %get-tuple-element.9, f32[3,1024]{1,0:T(4,128)S(1)} %bitcast.23), kind=kLoop, calls=%fused_computation.2 | loop fusion | flops 4718592 | bytes 11046912 | tf_op jit(solution)/shard_map/convert_element_type | solution.py:161
  22.9 0.9 multiply_convert_fusion
  23.8 10.9 %all-to-all-done.1.received = bf16[64,16,256]{2,1,0:T(8,128)(2,1)S(1)} async-done(((bf16[64,16,256]{2,1,0:T(8,128)(2,1)}), bf16[64,16,256]{2,1,0:T(8,128)(2,1)S(1)}, u32[]{:S(2)}, u32[]{:S(2)}) %all-to-all-start.1) | async-done | bytes 524320 | tf_op jit(solution)/shard_map/all_to_all | solution.py:154
  34.7 5.9 %all-to-all-start = ((bf16[64,16,256]{2,1,0:T(8,128)(2,1)}), bf16[64,16,256]{2,1,0:T(8,128)(2,1)S(1)}, u32[]{:S(2)}, u32[]{:S(2)}) async-start(bf16[64,16,256]{2,1,0:T(8,128)(2,1)} %bitcast.21), calls=%async_computation | async-start | bytes 1048576 | tf_op jit(solution)/shard_map/all_to_all | solution.py:163
  40.6 0.8 dynamic_slice.15.skip
  41.4 0.0 copy-done
  41.4 0.0 copy-done.2
  41.4 0.0 copy-done.3
  41.4 0.0 copy-start.1
  41.4 0.0 copy-start.4
  41.4 2.5 %shard_map.100.spectrum = f32[16,128,256]{2,1,0:T(8,128)S(1)} custom-call(bf16[64,16,256]{2,1,0:T(8,128)(2,1)S(1)} %all-to-all-done.1.received, bf16[256,256]{1,0:T(8,128)(2,1)S(1)} %copy-done.2, f32[2,128,128]{2,1,0:T(8,128)S(1)} %copy-done.3, bf16[2,256,256]{2,1,0:T(8,128)(2,1)S(1)} %copy-done), custom_call_target="tpu_custom_call" | custom-call | flops 2000000000 | bytes 4000000 | tf_op jit(solution)/shard_map/pallas_call | solution.py:131
  44.0 0.0 copy-start.5
  44.0 1.3 %copy-done.5 = f32[16,128,256]{2,1,0:T(8,128)} copy-done((f32[16,128,256]{2,1,0:T(8,128)}, f32[16,128,256]{2,1,0:T(8,128)S(1)}, u32[]{:S(2)}) %copy-start.5) | copy-done | bytes 2097176
  45.3 10.9 %all-to-all-done.received = bf16[64,16,256]{2,1,0:T(8,128)(2,1)S(1)} async-done(((bf16[64,16,256]{2,1,0:T(8,128)(2,1)}), bf16[64,16,256]{2,1,0:T(8,128)(2,1)S(1)}, u32[]{:S(2)}, u32[]{:S(2)}) %all-to-all-start) | async-done | bytes 524320 | tf_op jit(solution)/shard_map/all_to_all | solution.py:163
  56.1 0.0 copy-done.1
  56.1 0.0 copy-done.4
  56.2 0.0 copy-start.6
  56.2 1.6 %copy-done.6 = f32[16,128,256]{2,1,0:T(8,128)S(1)} copy-done((f32[16,128,256]{2,1,0:T(8,128)S(1)}, f32[16,128,256]{2,1,0:T(8,128)}, u32[]{:S(2)}) %copy-start.6) | copy-done | bytes 2097176
  57.7 5.6 %shard_map.101 = bf16[64,16,256]{2,1,0:T(8,128)(2,1)S(1)} custom-call(bf16[64,16,256]{2,1,0:T(8,128)(2,1)S(1)} %all-to-all-done.received, f32[16,128,256]{2,1,0:T(8,128)S(1)} %copy-done.6, f32[16]{0:T(128)S(1)} %dynamic_slice.15.skip, bf16[256,256]{1,0:T(8,128)(2,1)S(1)} %copy-done.2, f32[2,128,128]{2,1,0:T(8,128)S(1)} %copy-done.3, ...), custom_call_target="tpu_custom_call" | custom-call | flops 4000000000 | bytes 4000000 | tf_op jit(solution)/shard_map/pallas_call | solution.py:131
  63.3 20.9 %all_to_all.15 = bf16[64,16,256]{2,1,0:T(8,128)(2,1)S(1)} all-to-all(bf16[64,16,256]{2,1,0:T(8,128)(2,1)S(1)} %shard_map.101), channel_id=1, replica_groups=mesh['seq'=64,'mp'=4] {'seq'}, dimensions={0} | all-to-all | bytes 1048576 | tf_op jit(solution)/shard_map/all_to_all | solution.py:185
  84.2 0.2 fusion.23
  84.4 2.7 %collective-permute-start.2 = (bf16[1024,256]{1,0:T(8,128)(2,1)S(1)}, bf16[1024,256]{1,0:T(8,128)(2,1)S(1)}, u32[]{:S(2)}, u32[]{:S(2)}) collective-permute-start(bf16[1024,256]{1,0:T(8,128)(2,1)S(1)} %fusion.23), channel_id=1, source_target_pairs={{0,2},{1,3},{2,0},{3,1},{4,6},{5,7},{6,4},{7,5},{8,10},{9,11},{10,... | collective-permute-start | bytes 1572872 | tf_op jit(solution)/shard_map/ppermute | solution.py:191
  87.1 5.1 %collective-permute-start.1 = (bf16[1024,256]{1,0:T(8,128)(2,1)S(1)}, bf16[1024,256]{1,0:T(8,128)(2,1)S(1)}, u32[]{:S(2)}, u32[]{:S(2)}) collective-permute-start(bf16[1024,256]{1,0:T(8,128)(2,1)S(1)} %fusion.23), channel_id=1, source_target_pairs={{0,1},{1,0},{2,3},{3,2},{4,5},{5,4},{6,7},{7,6},{8,9},{9,8},{10,11... | collective-permute-start | bytes 1572872 | tf_op jit(solution)/shard_map/ppermute | solution.py:192
  92.2 2.3 %fusion.9 = f32[256,1024]{1,0:T(8,128)S(1)} fusion(bf16[1024,256]{1,0:T(8,128)(2,1)S(1)} %fusion.23, bf16[4096,1024]{1,0:T(8,128)(2,1)} %param.14, s32[]{:T(128)S(6)} %select_n.16), kind=kOutput, calls=%fused_computation.13 | convolution fusion | flops 536870912 | bytes 3670020 | tf_op jit(solution)/shard_map/dot_general | solution.py:196
  94.6 0.1 collective-permute-done.2
  94.7 5.7 %collective-permute-start.3 = (bf16[1024,256]{1,0:T(8,128)(2,1)S(1)}, bf16[1024,256]{1,0:T(8,128)(2,1)S(1)}, u32[]{:S(2)}, u32[]{:S(2)}) collective-permute-start(bf16[1024,256]{1,0:T(8,128)(2,1)S(1)} %collective-permute-done.2), channel_id=1, source_target_pairs={{0,1},{1,0},{2,3},{3,2},{4,5},{5,4},{6,7},{7,6},{8,9},{9,8},{10,11... | collective-permute-start | bytes 1572872 | tf_op jit(solution)/shard_map/ppermute | solution.py:201
  100.4 2.3 %fusion.5 = f32[256,1024]{1,0:T(8,128)S(1)} fusion(bf16[1024,256]{1,0:T(8,128)(2,1)S(1)} %collective-permute-done.2, bf16[4096,1024]{1,0:T(8,128)(2,1)} %param.14, s32[]{:T(128)S(6)} %select_n.18), kind=kOutput, calls=%fused_computation.9 | convolution fusion | flops 536870912 | bytes 3670020 | tf_op jit(solution)/shard_map/dot_general | solution.py:196
  102.7 0.0 collective-permute-done.1
  102.7 2.3 %fusion.14 = f32[256,1024]{1,0:T(8,128)S(1)} fusion(f32[256,1024]{1,0:T(8,128)S(1)} %fusion.5, f32[256,1024]{1,0:T(8,128)S(1)} %fusion.9, bf16[1024,256]{1,0:T(8,128)(2,1)S(1)} %collective-permute-done.1, bf16[4096,1024]{1,0:T(8,128)(2,1)} %param.14, s32[]{:T(128)S(6)} %select_n.17), kind=kOutput, calls=%fused_computation.16 | convolution fusion | flops 537395200 | bytes 5767172 | tf_op jit(solution)/shard_map/dot_general | solution.py:196
  105.1 0.0 collective-permute-done.3
  105.1 3.1 %fusion.20 = bf16[256,1024]{1,0:T(8,128)(2,1)} fusion(f32[256,1024]{1,0:T(8,128)S(1)} %fusion.14, bf16[1024,256]{1,0:T(8,128)(2,1)S(1)} %collective-permute-done.3, bf16[4096,1024]{1,0:T(8,128)(2,1)} %param.14, s32[]{:T(128)S(6)} %select_n.19), kind=kOutput, calls=%fused_computation.18 | convolution fusion | flops 537395200 | bytes 4194308 | tf_op jit(solution)/shard_map/dot_general | solution.py:196
  (3 shorter events, 0.0 us)
Async XLA Ops:
  0.0 18.6 %copy-start.7 = (bf16[3,1024,256]{2,1,0:T(8,128)(2,1)S(1)}, bf16[3,1024,256]{2,1,0:T(8,128)(2,1)}, u32[]{:S(2)}) copy-start(bf16[3,1024,256]{2,1,0:T(8,128)(2,1)} %param.10) | copy-start | bytes 4718596
  0.0 18.1 %copy-start.8 = (f32[3,3,1024]{2,1,0:T(4,128)S(1)}, f32[3,3,1024]{2,1,0:T(4,128)}, u32[]{:S(2)}) copy-start(f32[3,3,1024]{2,1,0:T(4,128)} %param.11) | copy-start | bytes 110596
  1.9 16.3 %collective-permute-start = (bf16[3,1024,2]{1,0,2:T(4,128)(2,1)S(1)}, bf16[3,1024,2]{1,0,2:T(4,128)(2,1)S(1)}, u32[]{:S(2)}, u32[]{:S(2)}) collective-permute-start(bf16[3,1024,2]{1,0,2:T(4,128)(2,1)S(1)} %copy.16), channel_id=1, source_target_pairs={{0,4},{4,8},{8,12},{12,16},{16,20},{20,24},{24,28},{28,32},{32,36}... | collective-permute-start | bytes 36872 | tf_op jit(solution)/shard_map/ppermute | solution.py:157
  6.3 28.4 %all-to-all-start.1 = ((bf16[64,16,256]{2,1,0:T(8,128)(2,1)}), bf16[64,16,256]{2,1,0:T(8,128)(2,1)S(1)}, u32[]{:S(2)}, u32[]{:S(2)}) async-start(bf16[64,16,256]{2,1,0:T(8,128)(2,1)} %bitcast.22), calls=%async_computation.1 | async-start | bytes 1048576 | tf_op jit(solution)/shard_map/all_to_all | solution.py:154
  19.6 21.8 %copy-start = (bf16[2,256,256]{2,1,0:T(8,128)(2,1)S(1)}, bf16[2,256,256]{2,1,0:T(8,128)(2,1)}, u32[]{:S(2)}) copy-start(bf16[2,256,256]{2,1,0:T(8,128)(2,1)} %constant.35.clone.forward2) | copy-start | bytes 786436
  19.6 21.8 %copy-start.2 = (bf16[256,256]{1,0:T(8,128)(2,1)S(1)}, bf16[256,256]{1,0:T(8,128)(2,1)}, u32[]{:S(2)}) copy-start(bf16[256,256]{1,0:T(8,128)(2,1)} %constant.33.clone.stage1) | copy-start | bytes 393220
  19.6 21.7 %copy-start.3 = (f32[2,128,128]{2,1,0:T(8,128)S(1)}, f32[2,128,128]{2,1,0:T(8,128)}, u32[]{:S(2)}) copy-start(f32[2,128,128]{2,1,0:T(8,128)} %constant.34.clone.turns) | copy-start | bytes 393220
  34.7 21.4 %all-to-all-start = ((bf16[64,16,256]{2,1,0:T(8,128)(2,1)}), bf16[64,16,256]{2,1,0:T(8,128)(2,1)S(1)}, u32[]{:S(2)}, u32[]{:S(2)}) async-start(bf16[64,16,256]{2,1,0:T(8,128)(2,1)} %bitcast.21), calls=%async_computation | async-start | bytes 1048576 | tf_op jit(solution)/shard_map/all_to_all | solution.py:163
  41.4 14.8 %copy-start.1 = (bf16[2,256,256]{2,1,0:T(8,128)(2,1)S(1)}, bf16[2,256,256]{2,1,0:T(8,128)(2,1)}, u32[]{:S(2)}) copy-start(bf16[2,256,256]{2,1,0:T(8,128)(2,1)} %constant.36.clone.inverse2) | copy-start | bytes 786436
  41.4 14.8 %copy-start.4 = (bf16[256,256]{1,0:T(8,128)(2,1)S(1)}, bf16[256,256]{1,0:T(8,128)(2,1)}, u32[]{:S(2)}) copy-start(bf16[256,256]{1,0:T(8,128)(2,1)} %constant.37.clone.inverse1) | copy-start | bytes 393220
  44.0 1.3 %copy-start.5 = (f32[16,128,256]{2,1,0:T(8,128)}, f32[16,128,256]{2,1,0:T(8,128)S(1)}, u32[]{:S(2)}) copy-start(f32[16,128,256]{2,1,0:T(8,128)S(1)} %shard_map.100.spectrum) | copy-start | bytes 6291460
  56.2 1.6 %copy-start.6 = (f32[16,128,256]{2,1,0:T(8,128)S(1)}, f32[16,128,256]{2,1,0:T(8,128)}, u32[]{:S(2)}) copy-start(f32[16,128,256]{2,1,0:T(8,128)} %copy-done.5) | copy-start | bytes 6291460
  84.4 10.3 %collective-permute-start.2 = (bf16[1024,256]{1,0:T(8,128)(2,1)S(1)}, bf16[1024,256]{1,0:T(8,128)(2,1)S(1)}, u32[]{:S(2)}, u32[]{:S(2)}) collective-permute-start(bf16[1024,256]{1,0:T(8,128)(2,1)S(1)} %fusion.23), channel_id=1, source_target_pairs={{0,2},{1,3},{2,0},{3,1},{4,6},{5,7},{6,4},{7,5},{8,10},{9,11},{10,... | collective-permute-start | bytes 1572872 | tf_op jit(solution)/shard_map/ppermute | solution.py:191
  87.1 15.6 %collective-permute-start.1 = (bf16[1024,256]{1,0:T(8,128)(2,1)S(1)}, bf16[1024,256]{1,0:T(8,128)(2,1)S(1)}, u32[]{:S(2)}, u32[]{:S(2)}) collective-permute-start(bf16[1024,256]{1,0:T(8,128)(2,1)S(1)} %fusion.23), channel_id=1, source_target_pairs={{0,1},{1,0},{2,3},{3,2},{4,5},{5,4},{6,7},{7,6},{8,9},{9,8},{10,11... | collective-permute-start | bytes 1572872 | tf_op jit(solution)/shard_map/ppermute | solution.py:192
  94.7 10.4 %collective-permute-start.3 = (bf16[1024,256]{1,0:T(8,128)(2,1)S(1)}, bf16[1024,256]{1,0:T(8,128)(2,1)S(1)}, u32[]{:S(2)}, u32[]{:S(2)}) collective-permute-start(bf16[1024,256]{1,0:T(8,128)(2,1)S(1)} %collective-permute-done.2), channel_id=1, source_target_pairs={{0,1},{1,0},{2,3},{3,2},{4,5},{5,4},{6,7},{7,6},{8,9},{9,8},{10,11... | collective-permute-start | bytes 1572872 | tf_op jit(solution)/shard_map/ppermute | solution.py:201
where the time goes:
time: 109 us; the launch traced here: 108 us
  starting transfers between devices  35.6 us (33%)
  waiting for transfers between devices  21.9 us (20%)
  blocking collectives  20.9 us (19%)
  matrix products  10.1 us (9%)
  Pallas kernels  8.12 us (7%)
  local copies, waits for them, and re-layouts  6.11 us (6%)
  other arithmetic  5.3 us (5%)
    all_to_all x1, blocking collectives, per_device(): lax.all_to_all(response, 'seq', split_axis=0, concat_axis=0, tiled=True)  20.9 us
    all_to_all x1, starting transfers between devices, per_device(): lax.all_to_all(long_filter.reshape(chunks), 'seq', split_axis=0, concat_a...  11.8 us
    all_to_all x1, waiting for transfers between devices, per_device(): lax.all_to_all(long_filter.reshape(chunks), 'seq', split_axis=0, concat_a...  10.9 us
    all_to_all x1, waiting for transfers between devices, per_device(): lax.all_to_all(gated.reshape(chunks), 'seq', split_axis=0, concat_axis=0,...  10.9 us
    dot_general x4, matrix products, part(): lax.dot_general(value, rows, (((0,), (0,)), ((), ())), preferred_element_...  10.1 us
    pallas_call x2, Pallas kernels, call(): pl.pallas_call(kernel, out_shape=out_shape, in_specs=specs, out_specs=pl....  8.12 us
    all_to_all x1, starting transfers between devices, per_device(): lax.all_to_all(gated.reshape(chunks), 'seq', split_axis=0, concat_axis=0,...  5.87 us
    ppermute x1, starting transfers between devices, per_device(): last = lax.ppermute(far, 'mp', [(m, m ^ 1) for m in range(4)])  5.7 us
  transfers between devices with their start and end apart: 6, of which 3 were waited for; matrix products, arithmetic and copies ran while one was open for 12% of the time, Pallas kernels for 2%

commit v1 on v0

v1 whole, which is shorter than its diff:
```python
import jax
import jax.numpy as jnp
import ml_dtypes
import numpy as np
from jax import lax
from jax.experimental import pallas as pl
from jax.experimental.pallas import tpu as pltpu
from jax.sharding import PartitionSpec as P

N1 = 128
N2 = 128
GROUP = 8
STRIP = 64


def split(table):
    high = table.astype(ml_dtypes.bfloat16)
    low = (table - high.astype(np.float64)).astype(ml_dtypes.bfloat16)
    return high, low


def dft_tables():
    order = np.concatenate([np.arange(0, N1, 2), np.arange(1, N1, 2)])
    k1 = np.arange(N1)
    first = 2.0 * np.pi * np.outer(k1 + 0.25, order) / N1
    stage1 = np.concatenate(split(np.concatenate([np.cos(first), -np.sin(first)], axis=0)), axis=1)
    turn = 2.0 * np.pi * np.outer(k1 + 0.25, np.arange(N2)) / (N1 * N2)
    turns = np.stack([np.cos(turn), np.sin(turn)]).astype(np.float32)
    second = 2.0 * np.pi * np.outer(np.arange(N2), np.arange(N2)) / N2
    cos, sin = np.cos(second), np.sin(second)
    high, low = split(np.block([[cos, -sin], [sin, cos]]))
    forward2 = np.concatenate([high, high, low], axis=0)
    high, low = split(np.block([[cos, sin], [-sin, cos]]))
    inverse2 = np.concatenate([high, high, low], axis=0)
    last = np.concatenate([np.cos(first.T), -np.sin(first.T)], axis=1) / (N1 * N2)
    inverse1 = np.concatenate(split(last), axis=0)
    return stage1, turns, forward2, inverse2, inverse1


def dot(a, b):
    return jnp.dot(a, b, preferred_element_type=jnp.float32)


def halves(value):
    high = value.astype(jnp.bfloat16)
    low = (value - high.astype(jnp.float32)).astype(jnp.bfloat16)
    return high, low


def wide_dot(value, table):
    high, low = halves(value)
    return dot(jnp.concatenate([high, low, high], axis=1), table)


def load_tile(flat, row, parts, stride):
    return jnp.concatenate([half[pl.ds(row, parts, stride=stride), :] for half in flat], axis=0)


def spectra_of(tiles, stage1, turns, forward2):
    cos, sin = turns[0], turns[1]
    turned = []
    for first in range(0, len(tiles), 2):
        pair = jnp.concatenate(tiles[first : first + 2], axis=1).astype(jnp.bfloat16)
        both = dot(stage1[...], jnp.concatenate([pair, pair], axis=0))
        for place in range(2):
            re = both[:N1, place * N2 : (place + 1) * N2]
            im = both[N1:, place * N2 : (place + 1) * N2]
            turned.append(jnp.concatenate([re * cos + im * sin, im * cos - re * sin], axis=1))
    return wide_dot(jnp.concatenate(turned, axis=0), forward2[...])


def conv_kernel(
    received, skip, stage1, turns, forward2, inverse2, inverse1, response,
    even, odd, out_even, out_odd, product, spectrum,
):
    parts, rows, _ = received.shape
    per_dev = rows // 2
    flat, out_flat = (even, odd), (out_even, out_odd)
    for half in range(2):
        flat[half][...] = (
            received[:, :, half * N2 : (half + 1) * N2].astype(jnp.float32).reshape(parts * rows, N2)
        )
    for start, spectra in ((per_dev, spectrum), (0, product)):
        for first in range(0, per_dev, GROUP):
            tiles = [load_tile(flat, start + first + c, parts, rows) for c in range(GROUP)]
            spectra[first * N1 : (first + GROUP) * N1, :] = spectra_of(tiles, stage1, turns, forward2)
    cos, sin = turns[0], turns[1]
    for first in range(0, per_dev, GROUP):
        span = slice(first * N1, (first + GROUP) * N1)
        sig_re, sig_im = product[span, :N2], product[span, N2:]
        ker_re, ker_im = spectrum[span, :N2], spectrum[span, N2:]
        multiplied = jnp.concatenate(
            [sig_re * ker_re - sig_im * ker_im, sig_re * ker_im + sig_im * ker_re], axis=1
        )
        back = wide_dot(multiplied, inverse2[...])
        for c in range(0, GROUP, 2):
            turned = []
            for place in (c, c + 1):
                re = back[place * N1 : (place + 1) * N1, :N2]
                im = back[place * N1 : (place + 1) * N1, N2:]
                turned.append(jnp.concatenate([re * cos - im * sin, re * sin + im * cos], axis=0))
            high, low = halves(jnp.concatenate(turned, axis=1))
            most = dot(inverse1[...], high)
            restored = most[:N1] + (most[N1:] + dot(inverse1[:N1, :], low))
            for place in range(2):
                channel = first + c + place
                tile = load_tile(flat, channel, parts, rows)
                out = restored[:, place * N2 : (place + 1) * N2] + skip[channel : channel + 1, :] * tile
                for half in range(2):
                    out_flat[half][pl.ds(channel, parts, stride=per_dev), :] = out[
                        half * parts : (half + 1) * parts
                    ]
    for half in range(2):
        response[:, :, half * N2 : (half + 1) * N2] = (
            out_flat[half][...].reshape(parts, per_dev, N2).astype(jnp.bfloat16)
        )


def tap_columns(taps, cols):
    rows = [taps[group] for group in range(3)] + [jnp.zeros((7, taps.shape[2]), jnp.float32)]
    columns = jnp.concatenate([row[:, cols] for row in rows], axis=0).T
    return [[columns[:, 3 * g + p : 3 * g + p + 1] for p in range(3)] for g in range(3)]


def weigh(tap, value, back1, back2):
    return (tap[0] * value + tap[1] * back1 + tap[2] * back2).astype(jnp.bfloat16)


def short_feature(left, right, tap, older, newer):
    left, right = left.astype(jnp.float32), right.astype(jnp.float32)
    lane = lax.broadcasted_iota(jnp.int32, left.shape, 1)
    left1, left2 = pltpu.roll(left, 1, 1), pltpu.roll(left, 2, 1)
    right1 = jnp.where(lane < 1, left1, pltpu.roll(right, 1, 1))
    right2 = jnp.where(lane < 2, left2, pltpu.roll(right, 2, 1))
    left1 = jnp.where(lane < 1, newer, left1)
    left2 = jnp.where(lane < 1, older, jnp.where(lane < 2, newer, left2))
    return weigh(tap, left, left1, left2), weigh(tap, right, right1, right2)


def gate(k, v):
    return (k.astype(jnp.float32) * v.astype(jnp.float32)).astype(jnp.bfloat16)


def strips(channels):
    return [slice(first, first + STRIP) for first in range(0, channels, STRIP)]


def edge_rows(pick, tiles):
    return [
        lax.dot_general(pick, tile, (((1,), (1,)), ((), ())), preferred_element_type=jnp.float32)
        for tile in tiles
    ]


def picker(lanes):
    row = lax.broadcasted_iota(jnp.int32, (16, N2), 0)
    lane = lax.broadcasted_iota(jnp.int32, (16, N2), 1)
    hit = jnp.zeros((16, N2), jnp.bool_)
    for place, wanted in enumerate(lanes):
        hit = hit | ((row == place) & (lane == wanted))
    return jnp.where(hit, 1.0, 0.0).astype(jnp.bfloat16)


def rim_kernel(projected, long_filter, short_taps, tails, pair, filter_out, taps, edge, arrived):
    groups, channels, _ = edge.shape
    moves = (
        (projected.at[:, :, N2:], edge),
        (projected.at[1:], pair),
        (long_filter, filter_out),
        (short_taps, taps),
    )
    copies = [
        pltpu.make_async_copy(source, target, arrived.at[place])
        for place, (source, target) in enumerate(moves)
    ]
    for copy in copies:
        copy.start()
    copies[0].wait()
    rows = edge_rows(picker((N2 - 2, N2 - 1)), [edge[group] for group in range(groups)])
    picked = [t[place : place + 1] for place in range(2) for t in rows]
    picked.append(jnp.zeros((2, channels), jnp.float32))
    tails[...] = jnp.concatenate(picked, axis=0).astype(jnp.bfloat16)
    for copy in copies[1:]:
        copy.wait()


def gate_kernel(pair, taps, gated, heads):
    _, channels, _ = pair.shape
    for first in range(0, channels, N1):
        columns = tap_columns(taps, slice(first, first + N1))
        for rows in strips(N1):
            place = slice(first + rows.start, first + rows.stop)
            k, v = [
                short_feature(
                    pair[group - 1, place, :N2],
                    pair[group - 1, place, N2:],
                    [column[rows] for column in columns[group]],
                    0.0,
                    0.0,
                )
                for group in (1, 2)
            ]
            gated[place, :N2] = gate(k[0], v[0])
            gated[place, N2:] = gate(k[1], v[1])
    rows = edge_rows(picker((0, 1)), [pair[group, :, :N2] for group in range(2)])
    picked = [t[place : place + 1] for place in range(2) for t in rows]
    picked.append(jnp.zeros((4, channels), jnp.float32))
    heads[...] = jnp.concatenate(picked, axis=0)


def mend_kernel(started, taps, rims, heads, long_filter, send):
    channels, tok_len = started.shape
    dests, sent, _ = send.shape
    per_dev = sent // 2
    ends = []
    for group in (1, 2):
        tap = [taps[group, place : place + 1, :] for place in range(3)]
        older = rims[group : group + 1, :].astype(jnp.float32)
        newer = rims[3 + group : 4 + group, :].astype(jnp.float32)
        zero, one = heads[group - 1 : group, :], heads[1 + group : 2 + group, :]
        ends.append(
            (
                (tap[0] * zero + tap[1] * newer + tap[2] * older).astype(jnp.bfloat16),
                (tap[0] * one + tap[1] * zero + tap[2] * newer).astype(jnp.bfloat16),
            )
        )
    first, second = [gate(k, v).astype(jnp.float32) for k, v in zip(*ends)]
    lane = lax.broadcasted_iota(jnp.int32, (N1, N2), 1)
    row = lax.broadcasted_iota(jnp.int32, (N1, N2), 0)
    for start in range(0, channels, N1):
        cols = slice(start, start + N1)
        to = slice(start // per_dev, (start + N1) // per_dev)
        spread = jnp.where(row == 0, first[:, cols], second[:, cols])
        value = started[cols, :N2].astype(jnp.float32)
        mended = jnp.where(lane < 2, spread.T, value).astype(jnp.bfloat16)
        send[to, :per_dev, :N2] = mended.reshape(N1 // per_dev, per_dev, N2)
    send[:, :per_dev, N2:] = started[:, N2:].reshape(dests, per_dev, tok_len - N2)
    send[:, per_dev:, :] = long_filter[...].reshape(dests, per_dev, tok_len)


def query_kernel(projected, taps, rims, query, held, arrived):
    channels, _ = held.shape
    copy = pltpu.make_async_copy(projected.at[0], held, arrived)
    copy.start()
    copy.wait()
    for first in range(0, channels, N1):
        cols = slice(first, first + N1)
        tap = tap_columns(taps, cols)[0]
        rims_t = jnp.concatenate(
            [rims[:, cols].astype(jnp.float32), jnp.zeros((8, N1), jnp.float32)], axis=0
        ).T
        for rows in strips(N1):
            place = slice(first + rows.start, first + rows.stop)
            query[place, :N2], query[place, N2:] = short_feature(
                held[place, :N2],
                held[place, N2:],
                [column[rows] for column in tap],
                rims_t[rows, 0:1],
                rims_t[rows, 3:4],
            )


def product_kernel(query, returned, turned):
    product = query[...].astype(jnp.float32) * returned[...].astype(jnp.float32)
    turned[...] = product.T.astype(jnp.bfloat16)


def own_matmul_kernel(mine, w_out, total, rest, held, arrived):
    me = lax.axis_index("mp")
    quarter = mine.shape[1]
    copies = []
    for flip in range(4):
        rows = pl.ds(pl.multiple_of((me ^ flip) * quarter, quarter), quarter)
        target = rest.at[pl.ds((flip - 1) * quarter, quarter), :] if flip else held
        copy = pltpu.make_async_copy(w_out.at[rows, :], target, arrived.at[flip])
        copy.start()
        copies.append(copy)
    copies[0].wait()
    total[...] = dot(mine[...], held[...])
    for copy in copies[1:]:
        copy.wait()


def cost(flops, moved):
    return pl.CostEstimate(flops=flops, bytes_accessed=moved, transcendentals=0)


def whole():
    return pl.BlockSpec(memory_space=pltpu.VMEM)


def in_hbm(value):
    return pltpu.with_memory_space_constraint(value, pltpu.HBM)


PARAMS = pltpu.CompilerParams(vmem_limit_bytes=32 * 2**20)


def per_device(projected, short_taps, long_filter, skip_gain, w_out):
    tok_len = projected.shape[2]
    quarter = projected.shape[1]
    seq_parts = lax.axis_size("seq")
    per_dev = quarter // seq_parts
    chunk = (seq_parts, per_dev, tok_len)
    stage1, turns, forward2, inverse2, inverse1 = [jnp.asarray(table) for table in dft_tables()]
    projected = in_hbm(projected)
    anywhere = pl.BlockSpec(memory_space=pl.ANY)

    def transposed(value):
        return lax.all_to_all(value, "seq", split_axis=0, concat_axis=0, tiled=True)

    tails, pair, filter_here, taps = pl.pallas_call(
        rim_kernel,
        out_shape=[
            jax.ShapeDtypeStruct((8, quarter), jnp.bfloat16),
            jax.ShapeDtypeStruct((2, quarter, tok_len), jnp.bfloat16),
            jax.ShapeDtypeStruct((quarter, tok_len), jnp.bfloat16),
            jax.ShapeDtypeStruct(short_taps.shape, jnp.float32),
        ],
        in_specs=[anywhere] * 3,
        out_specs=[whole()] * 4,
        scratch_shapes=[
            pltpu.VMEM((3, quarter, N2), jnp.bfloat16),
            pltpu.SemaphoreType.DMA((4,)),
        ],
        compiler_params=PARAMS,
        cost_estimate=cost(1000, 1000),
    )(projected, in_hbm(long_filter), in_hbm(short_taps))
    rims = lax.ppermute(tails, "seq", [(s, s + 1) for s in range(seq_parts - 1)])
    started, heads = pl.pallas_call(
        gate_kernel,
        out_shape=[
            jax.ShapeDtypeStruct((quarter, tok_len), jnp.bfloat16),
            jax.ShapeDtypeStruct((8, quarter), jnp.float32),
        ],
        in_specs=[whole()] * 2,
        out_specs=[whole()] * 2,
        compiler_params=PARAMS,
        cost_estimate=cost(1000, 1000),
    )(pair, taps)
    send = pl.pallas_call(
        mend_kernel,
        out_shape=jax.ShapeDtypeStruct((seq_parts, 2 * per_dev, tok_len), jnp.bfloat16),
        in_specs=[whole()] * 5,
        out_specs=whole(),
        compiler_params=PARAMS,
        cost_estimate=cost(1000, 1000),
    )(started, taps, rims, heads, filter_here)
    received = transposed(send)
    query = pl.pallas_call(
        query_kernel,
        out_shape=jax.ShapeDtypeStruct((quarter, tok_len), jnp.bfloat16),
        in_specs=[anywhere, whole(), whole()],
        out_specs=whole(),
        scratch_shapes=[pltpu.VMEM((quarter, tok_len), jnp.bfloat16), pltpu.SemaphoreType.DMA],
        compiler_params=PARAMS,
        cost_estimate=cost(5_000_000, 1_000_000),
    )(projected, taps, rims)
    received, query = lax.optimization_barrier((received, query))

    own_skip = lax.dynamic_slice_in_dim(skip_gain, lax.axis_index("seq") * per_dev, per_dev, 0)
    own_skip = jnp.broadcast_to(own_skip[:, None], (per_dev, N2))
    response = pl.pallas_call(
        conv_kernel,
        out_shape=jax.ShapeDtypeStruct(chunk, jnp.bfloat16),
        in_specs=[whole()] * 7,
        out_specs=whole(),
        scratch_shapes=[pltpu.VMEM((2 * quarter, N2), jnp.float32) for _ in range(2)]
        + [pltpu.VMEM((quarter, N2), jnp.float32) for _ in range(2)]
        + [pltpu.VMEM((per_dev * N1, 2 * N2), jnp.float32) for _ in range(2)],
        compiler_params=PARAMS,
        cost_estimate=cost(6_000_000_000, 4_000_000),
    )(received, own_skip, stage1, turns, forward2, inverse2, inverse1)
    returned = transposed(response)

    product = pl.pallas_call(
        product_kernel,
        out_shape=jax.ShapeDtypeStruct((tok_len, quarter), jnp.bfloat16),
        in_specs=[whole()] * 2,
        out_specs=whole(),
        compiler_params=PARAMS,
        cost_estimate=cost(1_000_000, 1_500_000),
    )(query, returned.reshape(quarter, tok_len))

    me = lax.axis_index("mp")
    to_far = [(m, m ^ 2) for m in range(4)]
    to_near = [(m, m ^ 1) for m in range(4)]

    far = lax.ppermute(product, "mp", to_far)
    near = lax.ppermute(product, "mp", to_near)
    out_len = w_out.shape[1]
    total, rest = pl.pallas_call(
        own_matmul_kernel,
        out_shape=[
            jax.ShapeDtypeStruct((tok_len, out_len), jnp.float32),
            jax.ShapeDtypeStruct((3 * quarter, out_len), jnp.bfloat16),
        ],
        in_specs=[whole(), anywhere],
        out_specs=[whole()] * 2,
        scratch_shapes=[pltpu.VMEM((quarter, out_len), jnp.bfloat16), pltpu.SemaphoreType.DMA((4,))],
        compiler_params=PARAMS,
        cost_estimate=cost(1000, 1000),
    )(product, in_hbm(w_out))
    total, rest, far = lax.optimization_barrier((total, rest, far))
    last = lax.ppermute(far, "mp", to_near)
    total = total + dot(far, rest[quarter : 2 * quarter])
    total = total + dot(near, rest[:quarter])
    return (total + dot(last, rest[2 * quarter :])).astype(jnp.bfloat16)


def solution(mesh):
    return jax.shard_map(
        per_device,
        mesh=mesh,
        in_specs=(
            P(None, "mp", "seq"),
            P(None, None, "mp"),
            P("mp", "seq"),
            P("mp"),
            P(None, "mp"),
        ),
        out_specs=P("seq", "mp"),
        check_vma=False,
    )
```

time: 109 us -> 96.4 us (0.88)
  Pallas kernels: 8.12 us -> 17.6 us
  matrix products: 10.1 us -> 2.99 us
  starting transfers between devices: 35.6 us -> 29.7 us
  other arithmetic: 5.3 us -> 0 us
  local copies, waits for them, and re-layouts: 6.11 us -> 0.86 us
  waiting for transfers between devices: 21.9 us -> 23 us
    pallas_call x2 -> x7, Pallas kernels: 8.12 us -> 17.6 us  [the longest x1 6.52 us: per_device(): pl.pallas_call(conv_kernel, out_shape=jax.ShapeDtypeStruct(chunk, jnp.bfl...]
    dot_general x4 -> x3, matrix products: 10.1 us -> 2.99 us  [dot(): return jnp.dot(a, b, preferred_element_type=jnp.float32)]
    convert_element_type x4 -> x0, other arithmetic: 5.3 us -> none  [the longest x1 3.22 us: per_device(): (features + short_taps[:, 2, :, None] * joined[:, :, 0:tok_len]).astype(j...]
    all_to_all x2 -> x1, starting transfers between devices: 17.7 us -> 12.7 us  [transposed(): return lax.all_to_all(value, 'seq', split_axis=0, concat_axis=0, tiled=True)]
    unnamed x21 -> x10, local copies, waits for them, and re-layouts: 3.35 us -> 0.02 us
    slice x2 -> x0, local copies, waits for them, and re-layouts: 1.57 us -> none  [the longest x1 1.54 us: per_device(): rim = projected[:, :, tok_len - 2:]]
    all_to_all x2 -> x1, waiting for transfers between devices: 21.8 us -> 22.9 us  [transposed(): return lax.all_to_all(value, 'seq', split_axis=0, concat_axis=0, tiled=True)]
  transfers between devices with their start and end apart: 6 -> 5, of which waited for: 3 -> 2; matrix products, arithmetic and copies ran while one was open for 12% -> 2% of each run, Pallas kernels for 2% -> 8%
where the time goes in v1:
time: 96.4 us; the launch traced here: 96 us
  starting transfers between devices  29.7 us (31%)
  waiting for transfers between devices  23 us (24%)
  blocking collectives  21.7 us (23%)
  Pallas kernels  17.6 us (18%)
  matrix products  2.99 us (3%)
    all_to_all x1, waiting for transfers between devices, transposed(): return lax.all_to_all(value, 'seq', split_axis=0, concat_axis=0, tiled=True)  22.9 us
    all_to_all x1, blocking collectives, transposed(): return lax.all_to_all(value, 'seq', split_axis=0, concat_axis=0, tiled=True)  21.7 us
    all_to_all x1, starting transfers between devices, transposed(): return lax.all_to_all(value, 'seq', split_axis=0, concat_axis=0, tiled=True)  12.7 us
    pallas_call x1, Pallas kernels, per_device(): pl.pallas_call(conv_kernel, out_shape=jax.ShapeDtypeStruct(chunk, jnp.bfl...  6.52 us
    ppermute x1, starting transfers between devices, per_device(): near = lax.ppermute(product, 'mp', to_near)  5.1 us
    ppermute x1, starting transfers between devices, per_device(): last = lax.ppermute(far, 'mp', to_near)  4.67 us
    ppermute x1, starting transfers between devices, per_device(): lax.ppermute(tails, 'seq', [(s, s + 1) for s in range(seq_parts - 1)])  4.37 us
    pallas_call x1, Pallas kernels, per_device(): pl.pallas_call(own_matmul_kernel, out_shape=[jax.ShapeDtypeStruct((tok_le...  3.5 us
  transfers between devices with their start and end apart: 5, of which 2 were waited for; matrix products, arithmetic and copies ran while one was open for 2% of the time, Pallas kernels for 8%

profile of v1, /device:TPU:1, one launch (start us, length us, event | category | flops | bytes accessed | tf_op | source)
XLA Modules:
  0.0 96.0 jit_solution(10110740607788522044)
XLA Ops:
  0.0 0.0 copy-start.2
  0.0 0.0 copy-start
  0.0 0.0 copy-start.1
  0.0 0.0 copy-start.3
  0.0 0.0 copy-start.4
  0.0 1.7 %shard_map.100 = (bf16[8,1024]{1,0:T(8,128)(2,1)S(1)}, bf16[2,1024,256]{2,1,0:T(8,128)(2,1)S(1)}, bf16[1024,256]{1,0:T(8,128)(2,1)S(1)}, f32[3,3,1024]{2,1,0:T(4,128)S(1)}) custom-call(bf16[3,1024,256]{2,1,0:T(8,128)(2,1)} %projected.3, bf16[1024,256]{1,0:T(8,128)(2,1)} %long_filter.1, f32[3,3,1024]{2,1,0:T(4,128)} %short_taps.1), custom_call_target="tpu_custom_call" | custom-call | flops 1000 | bytes 1000 | tf_op jit(solution)/shard_map/pallas_call | solution.py:312
  1.8 4.4 %collective-permute-start = (bf16[8,1024]{1,0:T(8,128)(2,1)S(1)}, bf16[8,1024]{1,0:T(8,128)(2,1)S(1)}, u32[]{:S(2)}, u32[]{:S(2)}) collective-permute-start(bf16[8,1024]{1,0:T(8,128)(2,1)S(1)} %get-tuple-element.21), channel_id=1, source_target_pairs={{0,4},{4,8},{8,12},{12,16},{16,20},{20,24},{24,28},{28,32},{32,36}... | collective-permute-start | bytes 49160 | tf_op jit(solution)/shard_map/ppermute | solution.py:329
  6.1 2.1 %shard_map.101 = (bf16[1024,256]{1,0:T(8,128)(2,1)S(1)}, f32[8,1024]{1,0:T(8,128)S(1)}) custom-call(bf16[2,1024,256]{2,1,0:T(8,128)(2,1)S(1)} %get-tuple-element.18.pair, f32[3,3,1024]{2,1,0:T(4,128)S(1)} %get-tuple-element.19.taps), custom_call_target="tpu_custom_call" | custom-call | flops 1000 | bytes 1000 | tf_op jit(solution)/shard_map/pallas_call | solution.py:330
  8.3 0.0 collective-permute-done.rims
  8.3 1.2 %shard_map.102 = bf16[64,32,256]{2,1,0:T(8,128)(2,1)} custom-call(bf16[1024,256]{1,0:T(8,128)(2,1)S(1)} %get-tuple-element.20.started, f32[3,3,1024]{2,1,0:T(4,128)S(1)} %get-tuple-element.19.taps, bf16[8,1024]{1,0:T(8,128)(2,1)S(1)} %collective-permute-done.rims, f32[8,1024]{1,0:T(8,128)S(1)} %get-tuple-element.22.heads, ...), custom_call_target="tpu_custom_call" | custom-call | flops 1000 | bytes 1000 | tf_op jit(solution)/shard_map/pallas_call | solution.py:341
  9.5 12.7 %all-to-all-start = ((bf16[64,32,256]{2,1,0:T(8,128)(2,1)}), bf16[64,32,256]{2,1,0:T(8,128)(2,1)S(1)}, u32[]{:S(2)}, u32[]{:S(2)}) async-start(bf16[64,32,256]{2,1,0:T(8,128)(2,1)} %shard_map.102), calls=%async_computation | async-start | bytes 2097152 | tf_op jit(solution)/shard_map/all_to_all | solution.py:310
  22.2 0.8 dynamic_slice.3
  22.9 2.4 %shard_map.103.query = bf16[1024,256]{1,0:T(8,128)(2,1)S(1)} custom-call(bf16[3,1024,256]{2,1,0:T(8,128)(2,1)} %projected.3, f32[3,3,1024]{2,1,0:T(4,128)S(1)} %get-tuple-element.19.taps, bf16[8,1024]{1,0:T(8,128)(2,1)S(1)} %collective-permute-done.rims), custom_call_target="tpu_custom_call" | custom-call | flops 5000000 | bytes 1000000 | tf_op jit(solution)/shard_map/pallas_call | solution.py:350
  25.3 22.9 %all-to-all-done.received = bf16[64,32,256]{2,1,0:T(8,128)(2,1)S(1)} async-done(((bf16[64,32,256]{2,1,0:T(8,128)(2,1)}), bf16[64,32,256]{2,1,0:T(8,128)(2,1)S(1)}, u32[]{:S(2)}, u32[]{:S(2)}) %all-to-all-start) | async-done | bytes 1048608 | tf_op jit(solution)/shard_map/all_to_all | solution.py:310
  48.2 0.1 broadcast_in_dim.2.skip
  48.2 0.0 copy-done.2
  48.2 0.0 copy-done
  48.2 0.0 copy-done.1
  48.3 0.0 copy-done.3
  48.3 0.0 copy-done.4
  48.3 6.5 %shard_map.104 = bf16[64,16,256]{2,1,0:T(8,128)(2,1)S(1)} custom-call(bf16[64,32,256]{2,1,0:T(8,128)(2,1)S(1)} %all-to-all-done.received, f32[16,128]{1,0:T(8,128)S(1)} %broadcast_in_dim.2.skip, bf16[256,256]{1,0:T(8,128)(2,1)S(1)} %copy-done.4, f32[2,128,128]{2,1,0:T(8,128)S(1)} %copy-done.3, bf16[768,256]{1,0:T(8,128)(2,1)S(1)} %copy-done.1, ...), custom_call_target="tpu_custom_call" | custom-call | flops 6000000000 | bytes 4000000 | tf_op jit(solution)/shard_map/pallas_call | solution.py:363
  54.8 21.7 %all_to_all.10 = bf16[64,16,256]{2,1,0:T(8,128)(2,1)S(1)} all-to-all(bf16[64,16,256]{2,1,0:T(8,128)(2,1)S(1)} %shard_map.104), channel_id=1, replica_groups=mesh['seq'=64,'mp'=4] {'seq'}, dimensions={0} | all-to-all | bytes 1048576 | tf_op jit(solution)/shard_map/all_to_all | solution.py:310
  76.5 0.2 shard_map.105.mine
  76.7 2.9 %collective-permute-start.1 = (bf16[256,1024]{1,0:T(8,128)(2,1)S(1)}, bf16[256,1024]{1,0:T(8,128)(2,1)S(1)}, u32[]{:S(2)}, u32[]{:S(2)}) collective-permute-start(bf16[256,1024]{1,0:T(8,128)(2,1)S(1)} %shard_map.105.mine), channel_id=1, source_target_pairs={{0,2},{1,3},{2,0},{3,1},{4,6},{5,7},{6,4},{7,5},{8,10},{9,11},{10,... | collective-permute-start | bytes 1572872 | tf_op jit(solution)/shard_map/ppermute | solution.py:389
  79.6 5.1 %collective-permute-start.2 = (bf16[256,1024]{1,0:T(8,128)(2,1)S(1)}, bf16[256,1024]{1,0:T(8,128)(2,1)S(1)}, u32[]{:S(2)}, u32[]{:S(2)}) collective-permute-start(bf16[256,1024]{1,0:T(8,128)(2,1)S(1)} %shard_map.105.mine), channel_id=1, source_target_pairs={{0,1},{1,0},{2,3},{3,2},{4,5},{5,4},{6,7},{7,6},{8,9},{9,8},{10,11... | collective-permute-start | bytes 1572872 | tf_op jit(solution)/shard_map/ppermute | solution.py:390
  84.7 3.5 %shard_map.106 = (f32[256,1024]{1,0:T(8,128)S(1)}, bf16[3072,1024]{1,0:T(8,128)(2,1)S(1)}) custom-call(bf16[256,1024]{1,0:T(8,128)(2,1)S(1)} %shard_map.105.mine, bf16[4096,1024]{1,0:T(8,128)(2,1)} %w_out.1), custom_call_target="tpu_custom_call" | custom-call | flops 1000 | bytes 1000 | tf_op jit(solution)/shard_map/pallas_call | solution.py:392
  88.2 0.0 collective-permute-done.1
  88.2 4.7 %collective-permute-start.3 = (bf16[256,1024]{1,0:T(8,128)(2,1)S(1)}, bf16[256,1024]{1,0:T(8,128)(2,1)S(1)}, u32[]{:S(2)}, u32[]{:S(2)}) collective-permute-start(bf16[256,1024]{1,0:T(8,128)(2,1)S(1)} %collective-permute-done.1), channel_id=1, source_target_pairs={{0,1},{1,0},{2,3},{3,2},{4,5},{5,4},{6,7},{7,6},{8,9},{9,8},{10,11... | collective-permute-start | bytes 1572872 | tf_op jit(solution)/shard_map/ppermute | solution.py:405
  92.9 0.7 fusion.4
  93.6 0.0 collective-permute-done.2
  93.6 0.7 fusion.2
  94.4 0.1 collective-permute-done.3
  94.5 1.6 %add_convert_fusion = bf16[256,1024]{1,0:T(8,128)(2,1)} fusion(f32[256,1024]{1,0:T(8,128)S(1)} %fusion.2, f32[256,1024]{1,0:T(8,128)S(1)} %get-tuple-element.28, f32[256,1024]{1,0:T(8,128)S(1)} %fusion.4, bf16[256,1024]{1,0:T(8,128)(2,1)S(1)} %collective-permute-done.3, bf16[3072,1024]{1,0:T(8,128)(2,1)S(1)} %get-tuple-element.30), kind=kOutput, calls=%fused_computation.6 | convolution fusion | flops 537919488 | bytes 6291456 | tf_op jit(solution)/shard_map/dot_general | solution.py:41
Async XLA Ops:
  0.0 48.2 %copy-start.2 = (bf16[256,256]{1,0:T(8,128)(2,1)S(1)}, bf16[256,256]{1,0:T(8,128)(2,1)}, u32[]{:S(2)}) copy-start(bf16[256,256]{1,0:T(8,128)(2,1)} %constant.26.clone.inverse1) | copy-start | bytes 393220
  0.0 48.2 %copy-start = (bf16[768,256]{1,0:T(8,128)(2,1)S(1)}, bf16[768,256]{1,0:T(8,128)(2,1)}, u32[]{:S(2)}) copy-start(bf16[768,256]{1,0:T(8,128)(2,1)} %constant.25.clone.inverse2) | copy-start | bytes 1179652
  0.0 48.2 %copy-start.1 = (bf16[768,256]{1,0:T(8,128)(2,1)S(1)}, bf16[768,256]{1,0:T(8,128)(2,1)}, u32[]{:S(2)}) copy-start(bf16[768,256]{1,0:T(8,128)(2,1)} %constant.24.clone.forward2) | copy-start | bytes 1179652
  0.0 48.2 %copy-start.3 = (f32[2,128,128]{2,1,0:T(8,128)S(1)}, f32[2,128,128]{2,1,0:T(8,128)}, u32[]{:S(2)}) copy-start(f32[2,128,128]{2,1,0:T(8,128)} %constant.23.clone.turns) | copy-start | bytes 393220
  0.0 48.2 %copy-start.4 = (bf16[256,256]{1,0:T(8,128)(2,1)S(1)}, bf16[256,256]{1,0:T(8,128)(2,1)}, u32[]{:S(2)}) copy-start(bf16[256,256]{1,0:T(8,128)(2,1)} %constant.22.clone.stage1) | copy-start | bytes 393220
  1.8 6.5 %collective-permute-start = (bf16[8,1024]{1,0:T(8,128)(2,1)S(1)}, bf16[8,1024]{1,0:T(8,128)(2,1)S(1)}, u32[]{:S(2)}, u32[]{:S(2)}) collective-permute-start(bf16[8,1024]{1,0:T(8,128)(2,1)S(1)} %get-tuple-element.21), channel_id=1, source_target_pairs={{0,4},{4,8},{8,12},{12,16},{16,20},{20,24},{24,28},{28,32},{32,36}... | collective-permute-start | bytes 49160 | tf_op jit(solution)/shard_map/ppermute | solution.py:329
  9.5 38.7 %all-to-all-start = ((bf16[64,32,256]{2,1,0:T(8,128)(2,1)}), bf16[64,32,256]{2,1,0:T(8,128)(2,1)S(1)}, u32[]{:S(2)}, u32[]{:S(2)}) async-start(bf16[64,32,256]{2,1,0:T(8,128)(2,1)} %shard_map.102), calls=%async_computation | async-start | bytes 2097152 | tf_op jit(solution)/shard_map/all_to_all | solution.py:310
  76.7 11.5 %collective-permute-start.1 = (bf16[256,1024]{1,0:T(8,128)(2,1)S(1)}, bf16[256,1024]{1,0:T(8,128)(2,1)S(1)}, u32[]{:S(2)}, u32[]{:S(2)}) collective-permute-start(bf16[256,1024]{1,0:T(8,128)(2,1)S(1)} %shard_map.105.mine), channel_id=1, source_target_pairs={{0,2},{1,3},{2,0},{3,1},{4,6},{5,7},{6,4},{7,5},{8,10},{9,11},{10,... | collective-permute-start | bytes 1572872 | tf_op jit(solution)/shard_map/ppermute | solution.py:389
  79.6 14.0 %collective-permute-start.2 = (bf16[256,1024]{1,0:T(8,128)(2,1)S(1)}, bf16[256,1024]{1,0:T(8,128)(2,1)S(1)}, u32[]{:S(2)}, u32[]{:S(2)}) collective-permute-start(bf16[256,1024]{1,0:T(8,128)(2,1)S(1)} %shard_map.105.mine), channel_id=1, source_target_pairs={{0,1},{1,0},{2,3},{3,2},{4,5},{5,4},{6,7},{7,6},{8,9},{9,8},{10,11... | collective-permute-start | bytes 1572872 | tf_op jit(solution)/shard_map/ppermute | solution.py:390
  88.2 6.2 %collective-permute-start.3 = (bf16[256,1024]{1,0:T(8,128)(2,1)S(1)}, bf16[256,1024]{1,0:T(8,128)(2,1)S(1)}, u32[]{:S(2)}, u32[]{:S(2)}) collective-permute-start(bf16[256,1024]{1,0:T(8,128)(2,1)S(1)} %collective-permute-done.1), channel_id=1, source_target_pairs={{0,1},{1,0},{2,3},{3,2},{4,5},{5,4},{6,7},{7,6},{8,9},{9,8},{10,11... | collective-permute-start | bytes 1572872 | tf_op jit(solution)/shard_map/ppermute | solution.py:405

commit v2 on v1

--- a/solution.py
+++ b/solution.py
@@ -9,7 +9,8 @@
 
 N1 = 128
 N2 = 128
-GROUP = 8
+GROUP = 16
+GAP = 8
 STRIP = 64
 
 
@@ -49,7 +50,9 @@
 
 def wide_dot(value, table):
     high, low = halves(value)
-    return dot(jnp.concatenate([high, low, high], axis=1), table)
+    wide = jnp.concatenate([high, low, high], axis=1)
+    middle = wide.shape[0] // 2
+    return jnp.concatenate([dot(wide[:middle], table), dot(wide[middle:], table)], axis=0)
 
 
 def load_tile(flat, row, parts, stride):
@@ -76,13 +79,16 @@
     parts, rows, _ = received.shape
     per_dev = rows // 2
     flat, out_flat = (even, odd), (out_even, out_odd)
+    lanes = [slice(half * N2, (half + 1) * N2) for half in range(2)]
+    in_step, out_step = rows + GAP, per_dev + GAP
     for half in range(2):
-        flat[half][...] = (
-            received[:, :, half * N2 : (half + 1) * N2].astype(jnp.float32).reshape(parts * rows, N2)
-        )
+        for part in range(parts):
+            flat[half][part * in_step : part * in_step + rows, :] = received[
+                part, :, lanes[half]
+            ].astype(jnp.float32)
     for start, spectra in ((per_dev, spectrum), (0, product)):
         for first in range(0, per_dev, GROUP):
-            tiles = [load_tile(flat, start + first + c, parts, rows) for c in range(GROUP)]
+            tiles = [load_tile(flat, start + first + c, parts, in_step) for c in range(GROUP)]
             spectra[first * N1 : (first + GROUP) * N1, :] = spectra_of(tiles, stage1, turns, forward2)
     cos, sin = turns[0], turns[1]
     for first in range(0, per_dev, GROUP):
@@ -104,16 +110,16 @@
             restored = most[:N1] + (most[N1:] + dot(inverse1[:N1, :], low))
             for place in range(2):
                 channel = first + c + place
-                tile = load_tile(flat, channel, parts, rows)
-                out = restored[:, place * N2 : (place + 1) * N2] + skip[channel : channel + 1, :] * tile
+                out = restored[:, place * N2 : (place + 1) * N2]
                 for half in range(2):
-                    out_flat[half][pl.ds(channel, parts, stride=per_dev), :] = out[
+                    out_flat[half][pl.ds(channel, parts, stride=out_step), :] = out[
                         half * parts : (half + 1) * parts
                     ]
     for half in range(2):
-        response[:, :, half * N2 : (half + 1) * N2] = (
-            out_flat[half][...].reshape(parts, per_dev, N2).astype(jnp.bfloat16)
-        )
+        for part in range(parts):
+            direct = skip[...] * received[part, :per_dev, lanes[half]].astype(jnp.float32)
+            convolved = out_flat[half][part * out_step : part * out_step + per_dev, :]
+            response[part, :, lanes[half]] = (convolved + direct).astype(jnp.bfloat16)
 
 
 def tap_columns(taps, cols):
@@ -208,10 +214,21 @@
     heads[...] = jnp.concatenate(picked, axis=0)
 
 
-def mend_kernel(started, taps, rims, heads, long_filter, send):
-    channels, tok_len = started.shape
-    dests, sent, _ = send.shape
-    per_dev = sent // 2
+def mend_kernel(started, taps, rims, heads, long_filter, send, edge, arrived):
+    dests, per_dev, _ = edge.shape
+    channels = dests * per_dev
+    copies = [
+        pltpu.make_async_copy(
+            started.reshape(dests, per_dev, 2 * N2).at[:, :, N2:],
+            send.at[:, :per_dev, N2:],
+            arrived.at[0],
+        ),
+        pltpu.make_async_copy(
+            long_filter.reshape(dests, per_dev, 2 * N2), send.at[:, per_dev:, :], arrived.at[1]
+        ),
+    ]
+    for copy in copies:
+        copy.start()
     ends = []
     for group in (1, 2):
         tap = [taps[group, place : place + 1, :] for place in range(3)]
@@ -233,9 +250,11 @@
         spread = jnp.where(row == 0, first[:, cols], second[:, cols])
         value = started[cols, :N2].astype(jnp.float32)
         mended = jnp.where(lane < 2, spread.T, value).astype(jnp.bfloat16)
-        send[to, :per_dev, :N2] = mended.reshape(N1 // per_dev, per_dev, N2)
-    send[:, :per_dev, N2:] = started[:, N2:].reshape(dests, per_dev, tok_len - N2)
-    send[:, per_dev:, :] = long_filter[...].reshape(dests, per_dev, tok_len)
+        edge[to, :, :] = mended.reshape(N1 // per_dev, per_dev, N2)
+    copies.append(pltpu.make_async_copy(edge, send.at[:, :per_dev, :N2], arrived.at[2]))
+    copies[2].start()
+    for copy in copies:
+        copy.wait()
 
 
 def query_kernel(projected, taps, rims, query, held, arrived):
@@ -281,6 +300,23 @@
         copy.wait()
 
 
+def last_matmul_kernel(total, value, rest, mixed, held, arrived):
+    tokens, out_len = held.shape
+    quarter = value.shape[1]
+    step = out_len // 4
+    copies = []
+    for place in range(4):
+        cols = slice(place * step, (place + 1) * step)
+        held[:, cols] = (total[:, cols] + dot(value[...], rest[2 * quarter :, cols])).astype(
+            jnp.bfloat16
+        )
+        copy = pltpu.make_async_copy(held.at[:, cols], mixed.at[:, cols], arrived.at[place])
+        copy.start()
+        copies.append(copy)
+    for copy in copies:
+        copy.wait()
+
+
 def cost(flops, moved):
     return pl.CostEstimate(flops=flops, bytes_accessed=moved, transcendentals=0)
 
@@ -342,7 +378,11 @@
         mend_kernel,
         out_shape=jax.ShapeDtypeStruct((seq_parts, 2 * per_dev, tok_len), jnp.bfloat16),
         in_specs=[whole()] * 5,
-        out_specs=whole(),
+        out_specs=anywhere,
+        scratch_shapes=[
+            pltpu.VMEM((seq_parts, per_dev, N2), jnp.bfloat16),
+            pltpu.SemaphoreType.DMA((3,)),
+        ],
         compiler_params=PARAMS,
         cost_estimate=cost(1000, 1000),
     )(started, taps, rims, heads, filter_here)
@@ -365,8 +405,10 @@
         out_shape=jax.ShapeDtypeStruct(chunk, jnp.bfloat16),
         in_specs=[whole()] * 7,
         out_specs=whole(),
-        scratch_shapes=[pltpu.VMEM((2 * quarter, N2), jnp.float32) for _ in range(2)]
-        + [pltpu.VMEM((quarter, N2), jnp.float32) for _ in range(2)]
+        scratch_shapes=[
+            pltpu.VMEM((seq_parts * (rows + GAP), N2), jnp.float32)
+            for rows in (2 * per_dev, 2 * per_dev, per_dev, per_dev)
+        ]
         + [pltpu.VMEM((per_dev * N1, 2 * N2), jnp.float32) for _ in range(2)],
         compiler_params=PARAMS,
         cost_estimate=cost(6_000_000_000, 4_000_000),
@@ -405,7 +447,18 @@
     last = lax.ppermute(far, "mp", to_near)
     total = total + dot(far, rest[quarter : 2 * quarter])
     total = total + dot(near, rest[:quarter])
-    return (total + dot(last, rest[2 * quarter :])).astype(jnp.bfloat16)
+    return pl.pallas_call(
+        last_matmul_kernel,
+        out_shape=jax.ShapeDtypeStruct((tok_len, out_len), jnp.bfloat16),
+        in_specs=[whole()] * 3,
+        out_specs=anywhere,
+        scratch_shapes=[
+            pltpu.VMEM((tok_len, out_len), jnp.bfloat16),
+            pltpu.SemaphoreType.DMA((4,)),
+        ],
+        compiler_params=PARAMS,
+        cost_estimate=cost(500_000_000, 4_000_000),
+    )(total, last, rest)
 
 
 def solution(mesh):

time: 96.4 us -> 93.7 us (0.972)
  matrix products: 2.99 us -> 1.43 us
    pallas_call x1, Pallas kernels: 6.52 us -> 4.27 us  [per_device(): pl.pallas_call(conv_kernel, out_shape=jax.ShapeDtypeStruct(chunk, jnp.bfl...]
    dot_general x3 -> x2, matrix products: 2.99 us -> 1.43 us  [dot(): return jnp.dot(a, b, preferred_element_type=jnp.float32)]
    pallas_call x0 -> x1, Pallas kernels: none -> 1.46 us  [per_device(): pl.pallas_call(last_matmul_kernel, out_shape=jax.ShapeDtypeStruct((tok_le...]
  transfers between devices with their start and end apart: 5 -> 5, of which waited for: 2 -> 2; matrix products, arithmetic and copies ran while one was open for 2% -> 2% of each run, Pallas kernels for 8% -> 9%
where the time goes in v2:
time: 93.7 us; the launch traced here: 93.4 us
  starting transfers between devices  29.6 us (32%)
  waiting for transfers between devices  23 us (25%)
  blocking collectives  21.7 us (23%)
  Pallas kernels  16.7 us (18%)
  matrix products  1.43 us (2%)
    all_to_all x1, waiting for transfers between devices, transposed(): return lax.all_to_all(value, 'seq', split_axis=0, concat_axis=0, tiled=True)  22.9 us
    all_to_all x1, blocking collectives, transposed(): return lax.all_to_all(value, 'seq', split_axis=0, concat_axis=0, tiled=True)  21.7 us
    all_to_all x1, starting transfers between devices, transposed(): return lax.all_to_all(value, 'seq', split_axis=0, concat_axis=0, tiled=True)  12.7 us
    ppermute x1, starting transfers between devices, per_device(): near = lax.ppermute(product, 'mp', to_near)  5.1 us
    ppermute x1, starting transfers between devices, per_device(): last = lax.ppermute(far, 'mp', to_near)  4.68 us
    ppermute x1, starting transfers between devices, per_device(): lax.ppermute(tails, 'seq', [(s, s + 1) for s in range(seq_parts - 1)])  4.37 us
    pallas_call x1, Pallas kernels, per_device(): pl.pallas_call(conv_kernel, out_shape=jax.ShapeDtypeStruct(chunk, jnp.bfl...  4.27 us
    pallas_call x1, Pallas kernels, per_device(): pl.pallas_call(own_matmul_kernel, out_shape=[jax.ShapeDtypeStruct((tok_le...  3.5 us
  transfers between devices with their start and end apart: 5, of which 2 were waited for; matrix products, arithmetic and copies ran while one was open for 2% of the time, Pallas kernels for 9%

profile of v2, /device:TPU:1, one launch (start us, length us, event | category | flops | bytes accessed | tf_op | source)
XLA Modules:
  0.0 93.4 jit_solution(13068512297567436615)
XLA Ops:
  0.0 0.0 copy-start.2
  0.0 0.0 copy-start
  0.0 0.0 copy-start.1
  0.0 0.0 copy-start.3
  0.0 0.0 copy-start.4
  0.0 1.7 %shard_map.100 = (bf16[8,1024]{1,0:T(8,128)(2,1)S(1)}, bf16[2,1024,256]{2,1,0:T(8,128)(2,1)S(1)}, bf16[1024,256]{1,0:T(8,128)(2,1)S(1)}, f32[3,3,1024]{2,1,0:T(4,128)S(1)}) custom-call(bf16[3,1024,256]{2,1,0:T(8,128)(2,1)} %projected.3, bf16[1024,256]{1,0:T(8,128)(2,1)} %long_filter.1, f32[3,3,1024]{2,1,0:T(4,128)} %short_taps.1), custom_call_target="tpu_custom_call" | custom-call | flops 1000 | bytes 1000 | tf_op jit(solution)/shard_map/pallas_call | solution.py:348
  1.8 4.4 %collective-permute-start = (bf16[8,1024]{1,0:T(8,128)(2,1)S(1)}, bf16[8,1024]{1,0:T(8,128)(2,1)S(1)}, u32[]{:S(2)}, u32[]{:S(2)}) collective-permute-start(bf16[8,1024]{1,0:T(8,128)(2,1)S(1)} %get-tuple-element.21), channel_id=1, source_target_pairs={{0,4},{4,8},{8,12},{12,16},{16,20},{20,24},{24,28},{28,32},{32,36}... | collective-permute-start | bytes 49160 | tf_op jit(solution)/shard_map/ppermute | solution.py:365
  6.1 2.1 %shard_map.101 = (bf16[1024,256]{1,0:T(8,128)(2,1)S(1)}, f32[8,1024]{1,0:T(8,128)S(1)}) custom-call(bf16[2,1024,256]{2,1,0:T(8,128)(2,1)S(1)} %get-tuple-element.18.pair, f32[3,3,1024]{2,1,0:T(4,128)S(1)} %get-tuple-element.19.taps), custom_call_target="tpu_custom_call" | custom-call | flops 1000 | bytes 1000 | tf_op jit(solution)/shard_map/pallas_call | solution.py:366
  8.3 0.0 collective-permute-done.rims
  8.3 1.0 %shard_map.102 = bf16[64,32,256]{2,1,0:T(8,128)(2,1)} custom-call(bf16[1024,256]{1,0:T(8,128)(2,1)S(1)} %get-tuple-element.20.started, f32[3,3,1024]{2,1,0:T(4,128)S(1)} %get-tuple-element.19.taps, bf16[8,1024]{1,0:T(8,128)(2,1)S(1)} %collective-permute-done.rims, f32[8,1024]{1,0:T(8,128)S(1)} %get-tuple-element.22.heads, ...), custom_call_target="tpu_custom_call" | custom-call | flops 1000 | bytes 1000 | tf_op jit(solution)/shard_map/pallas_call | solution.py:377
  9.3 12.7 %all-to-all-start = ((bf16[64,32,256]{2,1,0:T(8,128)(2,1)}), bf16[64,32,256]{2,1,0:T(8,128)(2,1)S(1)}, u32[]{:S(2)}, u32[]{:S(2)}) async-start(bf16[64,32,256]{2,1,0:T(8,128)(2,1)} %shard_map.102), calls=%async_computation | async-start | bytes 2097152 | tf_op jit(solution)/shard_map/all_to_all | solution.py:346
  22.0 0.8 dynamic_slice.3
  22.8 2.4 %shard_map.103.query = bf16[1024,256]{1,0:T(8,128)(2,1)S(1)} custom-call(bf16[3,1024,256]{2,1,0:T(8,128)(2,1)} %projected.3, f32[3,3,1024]{2,1,0:T(4,128)S(1)} %get-tuple-element.19.taps, bf16[8,1024]{1,0:T(8,128)(2,1)S(1)} %collective-permute-done.rims), custom_call_target="tpu_custom_call" | custom-call | flops 5000000 | bytes 1000000 | tf_op jit(solution)/shard_map/pallas_call | solution.py:390
  25.2 22.9 %all-to-all-done.received = bf16[64,32,256]{2,1,0:T(8,128)(2,1)S(1)} async-done(((bf16[64,32,256]{2,1,0:T(8,128)(2,1)}), bf16[64,32,256]{2,1,0:T(8,128)(2,1)S(1)}, u32[]{:S(2)}, u32[]{:S(2)}) %all-to-all-start) | async-done | bytes 1048608 | tf_op jit(solution)/shard_map/all_to_all | solution.py:346
  48.0 0.1 broadcast_in_dim.2.skip
  48.1 0.0 copy-done.2
  48.1 0.0 copy-done
  48.1 0.0 copy-done.1
  48.1 0.0 copy-done.3
  48.1 0.0 copy-done.4
  48.1 4.3 %shard_map.104 = bf16[64,16,256]{2,1,0:T(8,128)(2,1)S(1)} custom-call(bf16[64,32,256]{2,1,0:T(8,128)(2,1)S(1)} %all-to-all-done.received, f32[16,128]{1,0:T(8,128)S(1)} %broadcast_in_dim.2.skip, bf16[256,256]{1,0:T(8,128)(2,1)S(1)} %copy-done.4, f32[2,128,128]{2,1,0:T(8,128)S(1)} %copy-done.3, bf16[768,256]{1,0:T(8,128)(2,1)S(1)} %copy-done.1, ...), custom_call_target="tpu_custom_call" | custom-call | flops 6000000000 | bytes 4000000 | tf_op jit(solution)/shard_map/pallas_call | solution.py:403
  52.4 21.7 %all_to_all.10 = bf16[64,16,256]{2,1,0:T(8,128)(2,1)S(1)} all-to-all(bf16[64,16,256]{2,1,0:T(8,128)(2,1)S(1)} %shard_map.104), channel_id=1, replica_groups=mesh['seq'=64,'mp'=4] {'seq'}, dimensions={0} | all-to-all | bytes 1048576 | tf_op jit(solution)/shard_map/all_to_all | solution.py:346
  74.1 0.2 shard_map.105.mine
  74.4 2.7 %collective-permute-start.1 = (bf16[256,1024]{1,0:T(8,128)(2,1)S(1)}, bf16[256,1024]{1,0:T(8,128)(2,1)S(1)}, u32[]{:S(2)}, u32[]{:S(2)}) collective-permute-start(bf16[256,1024]{1,0:T(8,128)(2,1)S(1)} %shard_map.105.mine), channel_id=1, source_target_pairs={{0,2},{1,3},{2,0},{3,1},{4,6},{5,7},{6,4},{7,5},{8,10},{9,11},{10,... | collective-permute-start | bytes 1572872 | tf_op jit(solution)/shard_map/ppermute | solution.py:431
  77.1 5.1 %collective-permute-start.2 = (bf16[256,1024]{1,0:T(8,128)(2,1)S(1)}, bf16[256,1024]{1,0:T(8,128)(2,1)S(1)}, u32[]{:S(2)}, u32[]{:S(2)}) collective-permute-start(bf16[256,1024]{1,0:T(8,128)(2,1)S(1)} %shard_map.105.mine), channel_id=1, source_target_pairs={{0,1},{1,0},{2,3},{3,2},{4,5},{5,4},{6,7},{7,6},{8,9},{9,8},{10,11... | collective-permute-start | bytes 1572872 | tf_op jit(solution)/shard_map/ppermute | solution.py:432
  82.2 3.5 %shard_map.106 = (f32[256,1024]{1,0:T(8,128)S(1)}, bf16[3072,1024]{1,0:T(8,128)(2,1)S(1)}) custom-call(bf16[256,1024]{1,0:T(8,128)(2,1)S(1)} %shard_map.105.mine, bf16[4096,1024]{1,0:T(8,128)(2,1)} %w_out.1), custom_call_target="tpu_custom_call" | custom-call | flops 1000 | bytes 1000 | tf_op jit(solution)/shard_map/pallas_call | solution.py:434
  85.7 0.0 collective-permute-done.1
  85.7 4.7 %collective-permute-start.3 = (bf16[256,1024]{1,0:T(8,128)(2,1)S(1)}, bf16[256,1024]{1,0:T(8,128)(2,1)S(1)}, u32[]{:S(2)}, u32[]{:S(2)}) collective-permute-start(bf16[256,1024]{1,0:T(8,128)(2,1)S(1)} %collective-permute-done.1), channel_id=1, source_target_pairs={{0,1},{1,0},{2,3},{3,2},{4,5},{5,4},{6,7},{7,6},{8,9},{9,8},{10,11... | collective-permute-start | bytes 1572872 | tf_op jit(solution)/shard_map/ppermute | solution.py:447
  90.4 0.7 fusion.2
  91.1 0.0 collective-permute-done.2
  91.1 0.7 add_add_fusion.total
  91.8 0.1 collective-permute-done.3.value
  91.9 1.5 %shard_map.107 = bf16[256,1024]{1,0:T(8,128)(2,1)} custom-call(f32[256,1024]{1,0:T(8,128)S(1)} %add_add_fusion.total, bf16[256,1024]{1,0:T(8,128)(2,1)S(1)} %collective-permute-done.3.value, bf16[3072,1024]{1,0:T(8,128)(2,1)S(1)} %get-tuple-element.30.rest), custom_call_target="tpu_custom_call" | custom-call | flops 500000000 | bytes 4000000 | tf_op jit(solution)/shard_map/pallas_call | solution.py:450
Async XLA Ops:
  0.0 48.1 %copy-start.2 = (bf16[256,256]{1,0:T(8,128)(2,1)S(1)}, bf16[256,256]{1,0:T(8,128)(2,1)}, u32[]{:S(2)}) copy-start(bf16[256,256]{1,0:T(8,128)(2,1)} %constant.26.clone.inverse1) | copy-start | bytes 393220
  0.0 48.1 %copy-start = (bf16[768,256]{1,0:T(8,128)(2,1)S(1)}, bf16[768,256]{1,0:T(8,128)(2,1)}, u32[]{:S(2)}) copy-start(bf16[768,256]{1,0:T(8,128)(2,1)} %constant.25.clone.inverse2) | copy-start | bytes 1179652
  0.0 48.1 %copy-start.1 = (bf16[768,256]{1,0:T(8,128)(2,1)S(1)}, bf16[768,256]{1,0:T(8,128)(2,1)}, u32[]{:S(2)}) copy-start(bf16[768,256]{1,0:T(8,128)(2,1)} %constant.24.clone.forward2) | copy-start | bytes 1179652
  0.0 48.1 %copy-start.3 = (f32[2,128,128]{2,1,0:T(8,128)S(1)}, f32[2,128,128]{2,1,0:T(8,128)}, u32[]{:S(2)}) copy-start(f32[2,128,128]{2,1,0:T(8,128)} %constant.23.clone.turns) | copy-start | bytes 393220
  0.0 48.1 %copy-start.4 = (bf16[256,256]{1,0:T(8,128)(2,1)S(1)}, bf16[256,256]{1,0:T(8,128)(2,1)}, u32[]{:S(2)}) copy-start(bf16[256,256]{1,0:T(8,128)(2,1)} %constant.22.clone.stage1) | copy-start | bytes 393220
  1.8 6.5 %collective-permute-start = (bf16[8,1024]{1,0:T(8,128)(2,1)S(1)}, bf16[8,1024]{1,0:T(8,128)(2,1)S(1)}, u32[]{:S(2)}, u32[]{:S(2)}) collective-permute-start(bf16[8,1024]{1,0:T(8,128)(2,1)S(1)} %get-tuple-element.21), channel_id=1, source_target_pairs={{0,4},{4,8},{8,12},{12,16},{16,20},{20,24},{24,28},{28,32},{32,36}... | collective-permute-start | bytes 49160 | tf_op jit(solution)/shard_map/ppermute | solution.py:365
  9.3 38.7 %all-to-all-start = ((bf16[64,32,256]{2,1,0:T(8,128)(2,1)}), bf16[64,32,256]{2,1,0:T(8,128)(2,1)S(1)}, u32[]{:S(2)}, u32[]{:S(2)}) async-start(bf16[64,32,256]{2,1,0:T(8,128)(2,1)} %shard_map.102), calls=%async_computation | async-start | bytes 2097152 | tf_op jit(solution)/shard_map/all_to_all | solution.py:346
  74.4 11.3 %collective-permute-start.1 = (bf16[256,1024]{1,0:T(8,128)(2,1)S(1)}, bf16[256,1024]{1,0:T(8,128)(2,1)S(1)}, u32[]{:S(2)}, u32[]{:S(2)}) collective-permute-start(bf16[256,1024]{1,0:T(8,128)(2,1)S(1)} %shard_map.105.mine), channel_id=1, source_target_pairs={{0,2},{1,3},{2,0},{3,1},{4,6},{5,7},{6,4},{7,5},{8,10},{9,11},{10,... | collective-permute-start | bytes 1572872 | tf_op jit(solution)/shard_map/ppermute | solution.py:431
  77.1 14.0 %collective-permute-start.2 = (bf16[256,1024]{1,0:T(8,128)(2,1)S(1)}, bf16[256,1024]{1,0:T(8,128)(2,1)S(1)}, u32[]{:S(2)}, u32[]{:S(2)}) collective-permute-start(bf16[256,1024]{1,0:T(8,128)(2,1)S(1)} %shard_map.105.mine), channel_id=1, source_target_pairs={{0,1},{1,0},{2,3},{3,2},{4,5},{5,4},{6,7},{7,6},{8,9},{9,8},{10,11... | collective-permute-start | bytes 1572872 | tf_op jit(solution)/shard_map/ppermute | solution.py:432
  85.7 6.2 %collective-permute-start.3 = (bf16[256,1024]{1,0:T(8,128)(2,1)S(1)}, bf16[256,1024]{1,0:T(8,128)(2,1)S(1)}, u32[]{:S(2)}, u32[]{:S(2)}) collective-permute-start(bf16[256,1024]{1,0:T(8,128)(2,1)S(1)} %collective-permute-done.1), channel_id=1, source_target_pairs={{0,1},{1,0},{2,3},{3,2},{4,5},{5,4},{6,7},{7,6},{8,9},{9,8},{10,11... | collective-permute-start | bytes 1572872 | tf_op jit(solution)/shard_map/ppermute | solution.py:447

commit v3 on v2

--- a/solution.py
+++ b/solution.py
@@ -32,7 +32,7 @@
     high, low = split(np.block([[cos, -sin], [sin, cos]]))
     forward2 = np.concatenate([high, high, low], axis=0)
     high, low = split(np.block([[cos, sin], [-sin, cos]]))
-    inverse2 = np.concatenate([high, high, low], axis=0)
+    inverse2 = np.concatenate([high, low], axis=0)
     last = np.concatenate([np.cos(first.T), -np.sin(first.T)], axis=1) / (N1 * N2)
     inverse1 = np.concatenate(split(last), axis=0)
     return stage1, turns, forward2, inverse2, inverse1
@@ -48,11 +48,14 @@
     return high, low
 
 
+def split_dot(wide, table):
+    middle = wide.shape[0] // 2
+    return jnp.concatenate([dot(wide[:middle], table), dot(wide[middle:], table)], axis=0)
+
+
 def wide_dot(value, table):
     high, low = halves(value)
-    wide = jnp.concatenate([high, low, high], axis=1)
-    middle = wide.shape[0] // 2
-    return jnp.concatenate([dot(wide[:middle], table), dot(wide[middle:], table)], axis=0)
+    return split_dot(jnp.concatenate([high, low, high], axis=1), table)
 
 
 def load_tile(flat, row, parts, stride):
@@ -98,16 +101,16 @@
         multiplied = jnp.concatenate(
             [sig_re * ker_re - sig_im * ker_im, sig_re * ker_im + sig_im * ker_re], axis=1
         )
-        back = wide_dot(multiplied, inverse2[...])
+        held = multiplied.astype(jnp.bfloat16)
+        back = split_dot(jnp.concatenate([held, held], axis=1), inverse2[...])
         for c in range(0, GROUP, 2):
             turned = []
             for place in (c, c + 1):
                 re = back[place * N1 : (place + 1) * N1, :N2]
                 im = back[place * N1 : (place + 1) * N1, N2:]
                 turned.append(jnp.concatenate([re * cos - im * sin, re * sin + im * cos], axis=0))
-            high, low = halves(jnp.concatenate(turned, axis=1))
-            most = dot(inverse1[...], high)
-            restored = most[:N1] + (most[N1:] + dot(inverse1[:N1, :], low))
+            both = dot(inverse1[...], jnp.concatenate(turned, axis=1).astype(jnp.bfloat16))
+            restored = both[:N1] + both[N1:]
             for place in range(2):
                 channel = first + c + place
                 out = restored[:, place * N2 : (place + 1) * N2]

time: 93.7 us -> 93.2 us (level)
  no operation moved by 1% of the time
where the time goes in v3:
time: 93.2 us; the launch traced here: 92.8 us
  starting transfers between devices  29.6 us (32%)
  waiting for transfers between devices  23 us (25%)
  blocking collectives  21.7 us (23%)
  Pallas kernels  16.1 us (17%)
  matrix products  1.43 us (2%)
    all_to_all x1, waiting for transfers between devices, transposed(): return lax.all_to_all(value, 'seq', split_axis=0, concat_axis=0, tiled=True)  22.9 us
    all_to_all x1, blocking collectives, transposed(): return lax.all_to_all(value, 'seq', split_axis=0, concat_axis=0, tiled=True)  21.7 us
    all_to_all x1, starting transfers between devices, transposed(): return lax.all_to_all(value, 'seq', split_axis=0, concat_axis=0, tiled=True)  12.7 us
    ppermute x1, starting transfers between devices, per_device(): near = lax.ppermute(product, 'mp', to_near)  5.11 us
    ppermute x1, starting transfers between devices, per_device(): last = lax.ppermute(far, 'mp', to_near)  4.68 us
    ppermute x1, starting transfers between devices, per_device(): lax.ppermute(tails, 'seq', [(s, s + 1) for s in range(seq_parts - 1)])  4.37 us
    pallas_call x1, Pallas kernels, per_device(): pl.pallas_call(conv_kernel, out_shape=jax.ShapeDtypeStruct(chunk, jnp.bfl...  3.74 us
    pallas_call x1, Pallas kernels, per_device(): pl.pallas_call(own_matmul_kernel, out_shape=[jax.ShapeDtypeStruct((tok_le...  3.5 us
  transfers between devices with their start and end apart: 5, of which 2 were waited for; matrix products, arithmetic and copies ran while one was open for 2% of the time, Pallas kernels for 9%

profile of v3, /device:TPU:1, one launch (start us, length us, event | category | flops | bytes accessed | tf_op | source)
XLA Modules:
  0.0 92.8 jit_solution(3822600149482807326)
XLA Ops:
  0.0 0.0 copy-start.2
  0.0 0.0 copy-start.1
  0.0 0.0 copy-start
  0.0 0.0 copy-start.3
  0.0 0.0 copy-start.4
  0.0 1.7 %shard_map.100 = (bf16[8,1024]{1,0:T(8,128)(2,1)S(1)}, bf16[2,1024,256]{2,1,0:T(8,128)(2,1)S(1)}, bf16[1024,256]{1,0:T(8,128)(2,1)S(1)}, f32[3,3,1024]{2,1,0:T(4,128)S(1)}) custom-call(bf16[3,1024,256]{2,1,0:T(8,128)(2,1)} %projected.3, bf16[1024,256]{1,0:T(8,128)(2,1)} %long_filter.1, f32[3,3,1024]{2,1,0:T(4,128)} %short_taps.1), custom_call_target="tpu_custom_call" | custom-call | flops 1000 | bytes 1000 | tf_op jit(solution)/shard_map/pallas_call | solution.py:351
  1.8 4.4 %collective-permute-start = (bf16[8,1024]{1,0:T(8,128)(2,1)S(1)}, bf16[8,1024]{1,0:T(8,128)(2,1)S(1)}, u32[]{:S(2)}, u32[]{:S(2)}) collective-permute-start(bf16[8,1024]{1,0:T(8,128)(2,1)S(1)} %get-tuple-element.21), channel_id=1, source_target_pairs={{0,4},{4,8},{8,12},{12,16},{16,20},{20,24},{24,28},{28,32},{32,36}... | collective-permute-start | bytes 49160 | tf_op jit(solution)/shard_map/ppermute | solution.py:368
  6.1 2.1 %shard_map.101 = (bf16[1024,256]{1,0:T(8,128)(2,1)S(1)}, f32[8,1024]{1,0:T(8,128)S(1)}) custom-call(bf16[2,1024,256]{2,1,0:T(8,128)(2,1)S(1)} %get-tuple-element.18.pair, f32[3,3,1024]{2,1,0:T(4,128)S(1)} %get-tuple-element.19.taps), custom_call_target="tpu_custom_call" | custom-call | flops 1000 | bytes 1000 | tf_op jit(solution)/shard_map/pallas_call | solution.py:369
  8.3 0.0 collective-permute-done.rims
  8.3 1.0 %shard_map.102 = bf16[64,32,256]{2,1,0:T(8,128)(2,1)} custom-call(bf16[1024,256]{1,0:T(8,128)(2,1)S(1)} %get-tuple-element.20.started, f32[3,3,1024]{2,1,0:T(4,128)S(1)} %get-tuple-element.19.taps, bf16[8,1024]{1,0:T(8,128)(2,1)S(1)} %collective-permute-done.rims, f32[8,1024]{1,0:T(8,128)S(1)} %get-tuple-element.22.heads, ...), custom_call_target="tpu_custom_call" | custom-call | flops 1000 | bytes 1000 | tf_op jit(solution)/shard_map/pallas_call | solution.py:380
  9.3 12.7 %all-to-all-start = ((bf16[64,32,256]{2,1,0:T(8,128)(2,1)}), bf16[64,32,256]{2,1,0:T(8,128)(2,1)S(1)}, u32[]{:S(2)}, u32[]{:S(2)}) async-start(bf16[64,32,256]{2,1,0:T(8,128)(2,1)} %shard_map.102), calls=%async_computation | async-start | bytes 2097152 | tf_op jit(solution)/shard_map/all_to_all | solution.py:349
  22.0 0.8 dynamic_slice.3
  22.8 2.4 %shard_map.103.query = bf16[1024,256]{1,0:T(8,128)(2,1)S(1)} custom-call(bf16[3,1024,256]{2,1,0:T(8,128)(2,1)} %projected.3, f32[3,3,1024]{2,1,0:T(4,128)S(1)} %get-tuple-element.19.taps, bf16[8,1024]{1,0:T(8,128)(2,1)S(1)} %collective-permute-done.rims), custom_call_target="tpu_custom_call" | custom-call | flops 5000000 | bytes 1000000 | tf_op jit(solution)/shard_map/pallas_call | solution.py:393
  25.2 22.9 %all-to-all-done.received = bf16[64,32,256]{2,1,0:T(8,128)(2,1)S(1)} async-done(((bf16[64,32,256]{2,1,0:T(8,128)(2,1)}), bf16[64,32,256]{2,1,0:T(8,128)(2,1)S(1)}, u32[]{:S(2)}, u32[]{:S(2)}) %all-to-all-start) | async-done | bytes 1048608 | tf_op jit(solution)/shard_map/all_to_all | solution.py:349
  48.0 0.1 broadcast_in_dim.2.skip
  48.1 0.0 copy-done.2
  48.1 0.0 copy-done.1
  48.1 0.0 copy-done
  48.1 0.0 copy-done.3
  48.1 0.0 copy-done.4
  48.1 3.7 %shard_map.104 = bf16[64,16,256]{2,1,0:T(8,128)(2,1)S(1)} custom-call(bf16[64,32,256]{2,1,0:T(8,128)(2,1)S(1)} %all-to-all-done.received, f32[16,128]{1,0:T(8,128)S(1)} %broadcast_in_dim.2.skip, bf16[256,256]{1,0:T(8,128)(2,1)S(1)} %copy-done.4, f32[2,128,128]{2,1,0:T(8,128)S(1)} %copy-done.3, bf16[768,256]{1,0:T(8,128)(2,1)S(1)} %copy-done, ...), custom_call_target="tpu_custom_call" | custom-call | flops 6000000000 | bytes 4000000 | tf_op jit(solution)/shard_map/pallas_call | solution.py:406
  51.9 21.7 %all_to_all.10 = bf16[64,16,256]{2,1,0:T(8,128)(2,1)S(1)} all-to-all(bf16[64,16,256]{2,1,0:T(8,128)(2,1)S(1)} %shard_map.104), channel_id=1, replica_groups=mesh['seq'=64,'mp'=4] {'seq'}, dimensions={0} | all-to-all | bytes 1048576 | tf_op jit(solution)/shard_map/all_to_all | solution.py:349
  73.6 0.2 shard_map.105.mine
  73.8 2.7 %collective-permute-start.1 = (bf16[256,1024]{1,0:T(8,128)(2,1)S(1)}, bf16[256,1024]{1,0:T(8,128)(2,1)S(1)}, u32[]{:S(2)}, u32[]{:S(2)}) collective-permute-start(bf16[256,1024]{1,0:T(8,128)(2,1)S(1)} %shard_map.105.mine), channel_id=1, source_target_pairs={{0,2},{1,3},{2,0},{3,1},{4,6},{5,7},{6,4},{7,5},{8,10},{9,11},{10,... | collective-permute-start | bytes 1572872 | tf_op jit(solution)/shard_map/ppermute | solution.py:434
  76.5 5.1 %collective-permute-start.2 = (bf16[256,1024]{1,0:T(8,128)(2,1)S(1)}, bf16[256,1024]{1,0:T(8,128)(2,1)S(1)}, u32[]{:S(2)}, u32[]{:S(2)}) collective-permute-start(bf16[256,1024]{1,0:T(8,128)(2,1)S(1)} %shard_map.105.mine), channel_id=1, source_target_pairs={{0,1},{1,0},{2,3},{3,2},{4,5},{5,4},{6,7},{7,6},{8,9},{9,8},{10,11... | collective-permute-start | bytes 1572872 | tf_op jit(solution)/shard_map/ppermute | solution.py:435
  81.6 3.5 %shard_map.106 = (f32[256,1024]{1,0:T(8,128)S(1)}, bf16[3072,1024]{1,0:T(8,128)(2,1)S(1)}) custom-call(bf16[256,1024]{1,0:T(8,128)(2,1)S(1)} %shard_map.105.mine, bf16[4096,1024]{1,0:T(8,128)(2,1)} %w_out.1), custom_call_target="tpu_custom_call" | custom-call | flops 1000 | bytes 1000 | tf_op jit(solution)/shard_map/pallas_call | solution.py:437
  85.1 0.0 collective-permute-done.1
  85.2 4.7 %collective-permute-start.3 = (bf16[256,1024]{1,0:T(8,128)(2,1)S(1)}, bf16[256,1024]{1,0:T(8,128)(2,1)S(1)}, u32[]{:S(2)}, u32[]{:S(2)}) collective-permute-start(bf16[256,1024]{1,0:T(8,128)(2,1)S(1)} %collective-permute-done.1), channel_id=1, source_target_pairs={{0,1},{1,0},{2,3},{3,2},{4,5},{5,4},{6,7},{7,6},{8,9},{9,8},{10,11... | collective-permute-start | bytes 1572872 | tf_op jit(solution)/shard_map/ppermute | solution.py:450
  89.8 0.7 fusion.2
  90.5 0.0 collective-permute-done.2
  90.6 0.7 add_add_fusion.total
  91.3 0.1 collective-permute-done.3.value
  91.4 1.5 %shard_map.107 = bf16[256,1024]{1,0:T(8,128)(2,1)} custom-call(f32[256,1024]{1,0:T(8,128)S(1)} %add_add_fusion.total, bf16[256,1024]{1,0:T(8,128)(2,1)S(1)} %collective-permute-done.3.value, bf16[3072,1024]{1,0:T(8,128)(2,1)S(1)} %get-tuple-element.30.rest), custom_call_target="tpu_custom_call" | custom-call | flops 500000000 | bytes 4000000 | tf_op jit(solution)/shard_map/pallas_call | solution.py:453
Async XLA Ops:
  0.0 48.1 %copy-start.2 = (bf16[256,256]{1,0:T(8,128)(2,1)S(1)}, bf16[256,256]{1,0:T(8,128)(2,1)}, u32[]{:S(2)}) copy-start(bf16[256,256]{1,0:T(8,128)(2,1)} %constant.26.clone.inverse1) | copy-start | bytes 393220
  0.0 48.1 %copy-start.1 = (bf16[512,256]{1,0:T(8,128)(2,1)S(1)}, bf16[512,256]{1,0:T(8,128)(2,1)}, u32[]{:S(2)}) copy-start(bf16[512,256]{1,0:T(8,128)(2,1)} %constant.25.clone.inverse2) | copy-start | bytes 786436
  0.0 48.1 %copy-start = (bf16[768,256]{1,0:T(8,128)(2,1)S(1)}, bf16[768,256]{1,0:T(8,128)(2,1)}, u32[]{:S(2)}) copy-start(bf16[768,256]{1,0:T(8,128)(2,1)} %constant.24.clone.forward2) | copy-start | bytes 1179652
  0.0 48.1 %copy-start.3 = (f32[2,128,128]{2,1,0:T(8,128)S(1)}, f32[2,128,128]{2,1,0:T(8,128)}, u32[]{:S(2)}) copy-start(f32[2,128,128]{2,1,0:T(8,128)} %constant.23.clone.turns) | copy-start | bytes 393220
  0.0 48.1 %copy-start.4 = (bf16[256,256]{1,0:T(8,128)(2,1)S(1)}, bf16[256,256]{1,0:T(8,128)(2,1)}, u32[]{:S(2)}) copy-start(bf16[256,256]{1,0:T(8,128)(2,1)} %constant.22.clone.stage1) | copy-start | bytes 393220
  1.8 6.5 %collective-permute-start = (bf16[8,1024]{1,0:T(8,128)(2,1)S(1)}, bf16[8,1024]{1,0:T(8,128)(2,1)S(1)}, u32[]{:S(2)}, u32[]{:S(2)}) collective-permute-start(bf16[8,1024]{1,0:T(8,128)(2,1)S(1)} %get-tuple-element.21), channel_id=1, source_target_pairs={{0,4},{4,8},{8,12},{12,16},{16,20},{20,24},{24,28},{28,32},{32,36}... | collective-permute-start | bytes 49160 | tf_op jit(solution)/shard_map/ppermute | solution.py:368
  9.3 38.7 %all-to-all-start = ((bf16[64,32,256]{2,1,0:T(8,128)(2,1)}), bf16[64,32,256]{2,1,0:T(8,128)(2,1)S(1)}, u32[]{:S(2)}, u32[]{:S(2)}) async-start(bf16[64,32,256]{2,1,0:T(8,128)(2,1)} %shard_map.102), calls=%async_computation | async-start | bytes 2097152 | tf_op jit(solution)/shard_map/all_to_all | solution.py:349
  73.8 11.3 %collective-permute-start.1 = (bf16[256,1024]{1,0:T(8,128)(2,1)S(1)}, bf16[256,1024]{1,0:T(8,128)(2,1)S(1)}, u32[]{:S(2)}, u32[]{:S(2)}) collective-permute-start(bf16[256,1024]{1,0:T(8,128)(2,1)S(1)} %shard_map.105.mine), channel_id=1, source_target_pairs={{0,2},{1,3},{2,0},{3,1},{4,6},{5,7},{6,4},{7,5},{8,10},{9,11},{10,... | collective-permute-start | bytes 1572872 | tf_op jit(solution)/shard_map/ppermute | solution.py:434
  76.5 14.0 %collective-permute-start.2 = (bf16[256,1024]{1,0:T(8,128)(2,1)S(1)}, bf16[256,1024]{1,0:T(8,128)(2,1)S(1)}, u32[]{:S(2)}, u32[]{:S(2)}) collective-permute-start(bf16[256,1024]{1,0:T(8,128)(2,1)S(1)} %shard_map.105.mine), channel_id=1, source_target_pairs={{0,1},{1,0},{2,3},{3,2},{4,5},{5,4},{6,7},{7,6},{8,9},{9,8},{10,11... | collective-permute-start | bytes 1572872 | tf_op jit(solution)/shard_map/ppermute | solution.py:435
  85.2 6.2 %collective-permute-start.3 = (bf16[256,1024]{1,0:T(8,128)(2,1)S(1)}, bf16[256,1024]{1,0:T(8,128)(2,1)S(1)}, u32[]{:S(2)}, u32[]{:S(2)}) collective-permute-start(bf16[256,1024]{1,0:T(8,128)(2,1)S(1)} %collective-permute-done.1), channel_id=1, source_target_pairs={{0,1},{1,0},{2,3},{3,2},{4,5},{5,4},{6,7},{7,6},{8,9},{9,8},{10,11... | collective-permute-start | bytes 1572872 | tf_op jit(solution)/shard_map/ppermute | solution.py:450

commit v4 on v2

--- a/solution.py
+++ b/solution.py
@@ -167,12 +167,11 @@
     return jnp.where(hit, 1.0, 0.0).astype(jnp.bfloat16)
 
 
-def rim_kernel(projected, long_filter, short_taps, tails, pair, filter_out, taps, edge, arrived):
+def rim_kernel(projected, short_taps, tails, pair, taps, edge, arrived):
     groups, channels, _ = edge.shape
     moves = (
         (projected.at[:, :, N2:], edge),
         (projected.at[1:], pair),
-        (long_filter, filter_out),
         (short_taps, taps),
     )
     copies = [
@@ -190,8 +189,10 @@
         copy.wait()
 
 
-def gate_kernel(pair, taps, gated, heads):
+def gate_kernel(pair, taps, long_filter, gated, heads, filter_out, arrived):
     _, channels, _ = pair.shape
+    copy = pltpu.make_async_copy(long_filter, filter_out, arrived)
+    copy.start()
     for first in range(0, channels, N1):
         columns = tap_columns(taps, slice(first, first + N1))
         for rows in strips(N1):
@@ -212,6 +213,7 @@
     picked = [t[place : place + 1] for place in range(2) for t in rows]
     picked.append(jnp.zeros((4, channels), jnp.float32))
     heads[...] = jnp.concatenate(picked, axis=0)
+    copy.wait()
 
 
 def mend_kernel(started, taps, rims, heads, long_filter, send, edge, arrived):
@@ -345,35 +347,36 @@
     def transposed(value):
         return lax.all_to_all(value, "seq", split_axis=0, concat_axis=0, tiled=True)
 
-    tails, pair, filter_here, taps = pl.pallas_call(
+    tails, pair, taps = pl.pallas_call(
         rim_kernel,
         out_shape=[
             jax.ShapeDtypeStruct((8, quarter), jnp.bfloat16),
             jax.ShapeDtypeStruct((2, quarter, tok_len), jnp.bfloat16),
-            jax.ShapeDtypeStruct((quarter, tok_len), jnp.bfloat16),
             jax.ShapeDtypeStruct(short_taps.shape, jnp.float32),
         ],
-        in_specs=[anywhere] * 3,
-        out_specs=[whole()] * 4,
+        in_specs=[anywhere] * 2,
+        out_specs=[whole()] * 3,
         scratch_shapes=[
             pltpu.VMEM((3, quarter, N2), jnp.bfloat16),
-            pltpu.SemaphoreType.DMA((4,)),
+            pltpu.SemaphoreType.DMA((3,)),
         ],
         compiler_params=PARAMS,
         cost_estimate=cost(1000, 1000),
-    )(projected, in_hbm(long_filter), in_hbm(short_taps))
+    )(projected, in_hbm(short_taps))
     rims = lax.ppermute(tails, "seq", [(s, s + 1) for s in range(seq_parts - 1)])
-    started, heads = pl.pallas_call(
+    started, heads, filter_here = pl.pallas_call(
         gate_kernel,
         out_shape=[
             jax.ShapeDtypeStruct((quarter, tok_len), jnp.bfloat16),
             jax.ShapeDtypeStruct((8, quarter), jnp.float32),
-        ],
-        in_specs=[whole()] * 2,
-        out_specs=[whole()] * 2,
+            jax.ShapeDtypeStruct((quarter, tok_len), jnp.bfloat16),
+        ],
+        in_specs=[whole(), whole(), anywhere],
+        out_specs=[whole()] * 3,
+        scratch_shapes=[pltpu.SemaphoreType.DMA],
         compiler_params=PARAMS,
         cost_estimate=cost(1000, 1000),
-    )(pair, taps)
+    )(pair, taps, in_hbm(long_filter))
     send = pl.pallas_call(
         mend_kernel,
         out_shape=jax.ShapeDtypeStruct((seq_parts, 2 * per_dev, tok_len), jnp.bfloat16),
@@ -396,6 +399,7 @@
         compiler_params=PARAMS,
         cost_estimate=cost(5_000_000, 1_000_000),
     )(projected, taps, rims)
+
     received, query = lax.optimization_barrier((received, query))
 
     own_skip = lax.dynamic_slice_in_dim(skip_gain, lax.axis_index("seq") * per_dev, per_dev, 0)

time: 93.7 us -> 93.6 us (level)
  no operation moved by 1% of the time
where the time goes in v4:
time: 93.6 us; the launch traced here: 93.2 us
  starting transfers between devices  29.5 us (32%)
  waiting for transfers between devices  23 us (25%)
  blocking collectives  21.7 us (23%)
  Pallas kernels  16.6 us (18%)
  matrix products  1.43 us (2%)
    all_to_all x1, waiting for transfers between devices, transposed(): return lax.all_to_all(value, 'seq', split_axis=0, concat_axis=0, tiled=True)  22.9 us
    all_to_all x1, blocking collectives, transposed(): return lax.all_to_all(value, 'seq', split_axis=0, concat_axis=0, tiled=True)  21.7 us
    all_to_all x1, starting transfers between devices, transposed(): return lax.all_to_all(value, 'seq', split_axis=0, concat_axis=0, tiled=True)  12.7 us
    ppermute x1, starting transfers between devices, per_device(): near = lax.ppermute(product, 'mp', to_near)  5.11 us
    ppermute x1, starting transfers between devices, per_device(): last = lax.ppermute(far, 'mp', to_near)  4.68 us
    ppermute x1, starting transfers between devices, per_device(): lax.ppermute(tails, 'seq', [(s, s + 1) for s in range(seq_parts - 1)])  4.37 us
    pallas_call x1, Pallas kernels, per_device(): pl.pallas_call(conv_kernel, out_shape=jax.ShapeDtypeStruct(chunk, jnp.bfl...  4.28 us
    pallas_call x1, Pallas kernels, per_device(): pl.pallas_call(own_matmul_kernel, out_shape=[jax.ShapeDtypeStruct((tok_le...  3.5 us
  transfers between devices with their start and end apart: 5, of which 2 were waited for; matrix products, arithmetic and copies ran while one was open for 2% of the time, Pallas kernels for 9%

profile of v4, /device:TPU:1, one launch (start us, length us, event | category | flops | bytes accessed | tf_op | source)
XLA Modules:
  0.0 93.2 jit_solution(8486835391363003180)
XLA Ops:
  0.0 0.0 copy-start.2
  0.0 0.0 copy-start
  0.0 0.0 copy-start.1
  0.0 0.0 copy-start.3
  0.0 0.0 copy-start.4
  0.0 1.6 %shard_map.100 = (bf16[8,1024]{1,0:T(8,128)(2,1)S(1)}, bf16[2,1024,256]{2,1,0:T(8,128)(2,1)S(1)}, f32[3,3,1024]{2,1,0:T(4,128)S(1)}) custom-call(bf16[3,1024,256]{2,1,0:T(8,128)(2,1)} %projected.3, f32[3,3,1024]{2,1,0:T(4,128)} %short_taps.1), custom_call_target="tpu_custom_call" | custom-call | flops 1000 | bytes 1000 | tf_op jit(solution)/shard_map/pallas_call | solution.py:350
  1.6 4.4 %collective-permute-start = (bf16[8,1024]{1,0:T(8,128)(2,1)S(1)}, bf16[8,1024]{1,0:T(8,128)(2,1)S(1)}, u32[]{:S(2)}, u32[]{:S(2)}) collective-permute-start(bf16[8,1024]{1,0:T(8,128)(2,1)S(1)} %get-tuple-element.21), channel_id=1, source_target_pairs={{0,4},{4,8},{8,12},{12,16},{16,20},{20,24},{24,28},{28,32},{32,36}... | collective-permute-start | bytes 49160 | tf_op jit(solution)/shard_map/ppermute | solution.py:366
  6.0 2.1 %shard_map.101 = (bf16[1024,256]{1,0:T(8,128)(2,1)S(1)}, f32[8,1024]{1,0:T(8,128)S(1)}, bf16[1024,256]{1,0:T(8,128)(2,1)S(1)}) custom-call(bf16[2,1024,256]{2,1,0:T(8,128)(2,1)S(1)} %get-tuple-element.18.pair, f32[3,3,1024]{2,1,0:T(4,128)S(1)} %get-tuple-element.19.taps, bf16[1024,256]{1,0:T(8,128)(2,1)} %long_filter.1), custom_call_target="tpu_custom_call" | custom-call | flops 1000 | bytes 1000 | tf_op jit(solution)/shard_map/pallas_call | solution.py:367
  8.1 0.0 collective-permute-done.rims
  8.2 1.0 %shard_map.102 = bf16[64,32,256]{2,1,0:T(8,128)(2,1)} custom-call(bf16[1024,256]{1,0:T(8,128)(2,1)S(1)} %get-tuple-element.20.started, f32[3,3,1024]{2,1,0:T(4,128)S(1)} %get-tuple-element.19.taps, bf16[8,1024]{1,0:T(8,128)(2,1)S(1)} %collective-permute-done.rims, f32[8,1024]{1,0:T(8,128)S(1)} %get-tuple-element.22.heads, ...), custom_call_target="tpu_custom_call" | custom-call | flops 1000 | bytes 1000 | tf_op jit(solution)/shard_map/pallas_call | solution.py:380
  9.2 12.7 %all-to-all-start = ((bf16[64,32,256]{2,1,0:T(8,128)(2,1)}), bf16[64,32,256]{2,1,0:T(8,128)(2,1)S(1)}, u32[]{:S(2)}, u32[]{:S(2)}) async-start(bf16[64,32,256]{2,1,0:T(8,128)(2,1)} %shard_map.102), calls=%async_computation | async-start | bytes 2097152 | tf_op jit(solution)/shard_map/all_to_all | solution.py:348
  21.9 0.8 dynamic_slice.3
  22.7 2.4 %shard_map.103.query = bf16[1024,256]{1,0:T(8,128)(2,1)S(1)} custom-call(bf16[3,1024,256]{2,1,0:T(8,128)(2,1)} %projected.3, f32[3,3,1024]{2,1,0:T(4,128)S(1)} %get-tuple-element.19.taps, bf16[8,1024]{1,0:T(8,128)(2,1)S(1)} %collective-permute-done.rims), custom_call_target="tpu_custom_call" | custom-call | flops 5000000 | bytes 1000000 | tf_op jit(solution)/shard_map/pallas_call | solution.py:393
  25.0 22.9 %all-to-all-done.received = bf16[64,32,256]{2,1,0:T(8,128)(2,1)S(1)} async-done(((bf16[64,32,256]{2,1,0:T(8,128)(2,1)}), bf16[64,32,256]{2,1,0:T(8,128)(2,1)S(1)}, u32[]{:S(2)}, u32[]{:S(2)}) %all-to-all-start) | async-done | bytes 1048608 | tf_op jit(solution)/shard_map/all_to_all | solution.py:348
  47.9 0.1 broadcast_in_dim.2.skip
  48.0 0.0 copy-done.2
  48.0 0.0 copy-done
  48.0 0.0 copy-done.1
  48.0 0.0 copy-done.3
  48.0 0.0 copy-done.4
  48.0 4.3 %shard_map.104 = bf16[64,16,256]{2,1,0:T(8,128)(2,1)S(1)} custom-call(bf16[64,32,256]{2,1,0:T(8,128)(2,1)S(1)} %all-to-all-done.received, f32[16,128]{1,0:T(8,128)S(1)} %broadcast_in_dim.2.skip, bf16[256,256]{1,0:T(8,128)(2,1)S(1)} %copy-done.4, f32[2,128,128]{2,1,0:T(8,128)S(1)} %copy-done.3, bf16[768,256]{1,0:T(8,128)(2,1)S(1)} %copy-done.1, ...), custom_call_target="tpu_custom_call" | custom-call | flops 6000000000 | bytes 4000000 | tf_op jit(solution)/shard_map/pallas_call | solution.py:407
  52.3 21.7 %all_to_all.10 = bf16[64,16,256]{2,1,0:T(8,128)(2,1)S(1)} all-to-all(bf16[64,16,256]{2,1,0:T(8,128)(2,1)S(1)} %shard_map.104), channel_id=1, replica_groups=mesh['seq'=64,'mp'=4] {'seq'}, dimensions={0} | all-to-all | bytes 1048576 | tf_op jit(solution)/shard_map/all_to_all | solution.py:348
  74.0 0.2 shard_map.105.mine
  74.2 2.7 %collective-permute-start.1 = (bf16[256,1024]{1,0:T(8,128)(2,1)S(1)}, bf16[256,1024]{1,0:T(8,128)(2,1)S(1)}, u32[]{:S(2)}, u32[]{:S(2)}) collective-permute-start(bf16[256,1024]{1,0:T(8,128)(2,1)S(1)} %shard_map.105.mine), channel_id=1, source_target_pairs={{0,2},{1,3},{2,0},{3,1},{4,6},{5,7},{6,4},{7,5},{8,10},{9,11},{10,... | collective-permute-start | bytes 1572872 | tf_op jit(solution)/shard_map/ppermute | solution.py:435
  76.9 5.1 %collective-permute-start.2 = (bf16[256,1024]{1,0:T(8,128)(2,1)S(1)}, bf16[256,1024]{1,0:T(8,128)(2,1)S(1)}, u32[]{:S(2)}, u32[]{:S(2)}) collective-permute-start(bf16[256,1024]{1,0:T(8,128)(2,1)S(1)} %shard_map.105.mine), channel_id=1, source_target_pairs={{0,1},{1,0},{2,3},{3,2},{4,5},{5,4},{6,7},{7,6},{8,9},{9,8},{10,11... | collective-permute-start | bytes 1572872 | tf_op jit(solution)/shard_map/ppermute | solution.py:436
  82.0 3.5 %shard_map.106 = (f32[256,1024]{1,0:T(8,128)S(1)}, bf16[3072,1024]{1,0:T(8,128)(2,1)S(1)}) custom-call(bf16[256,1024]{1,0:T(8,128)(2,1)S(1)} %shard_map.105.mine, bf16[4096,1024]{1,0:T(8,128)(2,1)} %w_out.1), custom_call_target="tpu_custom_call" | custom-call | flops 1000 | bytes 1000 | tf_op jit(solution)/shard_map/pallas_call | solution.py:438
  85.6 0.0 collective-permute-done.1
  85.6 4.7 %collective-permute-start.3 = (bf16[256,1024]{1,0:T(8,128)(2,1)S(1)}, bf16[256,1024]{1,0:T(8,128)(2,1)S(1)}, u32[]{:S(2)}, u32[]{:S(2)}) collective-permute-start(bf16[256,1024]{1,0:T(8,128)(2,1)S(1)} %collective-permute-done.1), channel_id=1, source_target_pairs={{0,1},{1,0},{2,3},{3,2},{4,5},{5,4},{6,7},{7,6},{8,9},{9,8},{10,11... | collective-permute-start | bytes 1572872 | tf_op jit(solution)/shard_map/ppermute | solution.py:451
  90.2 0.7 fusion.2
  91.0 0.0 collective-permute-done.2
  91.0 0.7 add_add_fusion.total
  91.7 0.1 collective-permute-done.3.value
  91.8 1.5 %shard_map.107 = bf16[256,1024]{1,0:T(8,128)(2,1)} custom-call(f32[256,1024]{1,0:T(8,128)S(1)} %add_add_fusion.total, bf16[256,1024]{1,0:T(8,128)(2,1)S(1)} %collective-permute-done.3.value, bf16[3072,1024]{1,0:T(8,128)(2,1)S(1)} %get-tuple-element.30.rest), custom_call_target="tpu_custom_call" | custom-call | flops 500000000 | bytes 4000000 | tf_op jit(solution)/shard_map/pallas_call | solution.py:454
Async XLA Ops:
  0.0 48.0 %copy-start.2 = (bf16[256,256]{1,0:T(8,128)(2,1)S(1)}, bf16[256,256]{1,0:T(8,128)(2,1)}, u32[]{:S(2)}) copy-start(bf16[256,256]{1,0:T(8,128)(2,1)} %constant.26.clone.inverse1) | copy-start | bytes 393220
  0.0 48.0 %copy-start = (bf16[768,256]{1,0:T(8,128)(2,1)S(1)}, bf16[768,256]{1,0:T(8,128)(2,1)}, u32[]{:S(2)}) copy-start(bf16[768,256]{1,0:T(8,128)(2,1)} %constant.25.clone.inverse2) | copy-start | bytes 1179652
  0.0 48.0 %copy-start.1 = (bf16[768,256]{1,0:T(8,128)(2,1)S(1)}, bf16[768,256]{1,0:T(8,128)(2,1)}, u32[]{:S(2)}) copy-start(bf16[768,256]{1,0:T(8,128)(2,1)} %constant.24.clone.forward2) | copy-start | bytes 1179652
  0.0 48.0 %copy-start.3 = (f32[2,128,128]{2,1,0:T(8,128)S(1)}, f32[2,128,128]{2,1,0:T(8,128)}, u32[]{:S(2)}) copy-start(f32[2,128,128]{2,1,0:T(8,128)} %constant.23.clone.turns) | copy-start | bytes 393220
  0.0 48.0 %copy-start.4 = (bf16[256,256]{1,0:T(8,128)(2,1)S(1)}, bf16[256,256]{1,0:T(8,128)(2,1)}, u32[]{:S(2)}) copy-start(bf16[256,256]{1,0:T(8,128)(2,1)} %constant.22.clone.stage1) | copy-start | bytes 393220
  1.6 6.5 %collective-permute-start = (bf16[8,1024]{1,0:T(8,128)(2,1)S(1)}, bf16[8,1024]{1,0:T(8,128)(2,1)S(1)}, u32[]{:S(2)}, u32[]{:S(2)}) collective-permute-start(bf16[8,1024]{1,0:T(8,128)(2,1)S(1)} %get-tuple-element.21), channel_id=1, source_target_pairs={{0,4},{4,8},{8,12},{12,16},{16,20},{20,24},{24,28},{28,32},{32,36}... | collective-permute-start | bytes 49160 | tf_op jit(solution)/shard_map/ppermute | solution.py:366
  9.2 38.7 %all-to-all-start = ((bf16[64,32,256]{2,1,0:T(8,128)(2,1)}), bf16[64,32,256]{2,1,0:T(8,128)(2,1)S(1)}, u32[]{:S(2)}, u32[]{:S(2)}) async-start(bf16[64,32,256]{2,1,0:T(8,128)(2,1)} %shard_map.102), calls=%async_computation | async-start | bytes 2097152 | tf_op jit(solution)/shard_map/all_to_all | solution.py:348
  74.2 11.3 %collective-permute-start.1 = (bf16[256,1024]{1,0:T(8,128)(2,1)S(1)}, bf16[256,1024]{1,0:T(8,128)(2,1)S(1)}, u32[]{:S(2)}, u32[]{:S(2)}) collective-permute-start(bf16[256,1024]{1,0:T(8,128)(2,1)S(1)} %shard_map.105.mine), channel_id=1, source_target_pairs={{0,2},{1,3},{2,0},{3,1},{4,6},{5,7},{6,4},{7,5},{8,10},{9,11},{10,... | collective-permute-start | bytes 1572872 | tf_op jit(solution)/shard_map/ppermute | solution.py:435
  76.9 14.0 %collective-permute-start.2 = (bf16[256,1024]{1,0:T(8,128)(2,1)S(1)}, bf16[256,1024]{1,0:T(8,128)(2,1)S(1)}, u32[]{:S(2)}, u32[]{:S(2)}) collective-permute-start(bf16[256,1024]{1,0:T(8,128)(2,1)S(1)} %shard_map.105.mine), channel_id=1, source_target_pairs={{0,1},{1,0},{2,3},{3,2},{4,5},{5,4},{6,7},{7,6},{8,9},{9,8},{10,11... | collective-permute-start | bytes 1572872 | tf_op jit(solution)/shard_map/ppermute | solution.py:436
  85.6 6.2 %collective-permute-start.3 = (bf16[256,1024]{1,0:T(8,128)(2,1)S(1)}, bf16[256,1024]{1,0:T(8,128)(2,1)S(1)}, u32[]{:S(2)}, u32[]{:S(2)}) collective-permute-start(bf16[256,1024]{1,0:T(8,128)(2,1)S(1)} %collective-permute-done.1), channel_id=1, source_target_pairs={{0,1},{1,0},{2,3},{3,2},{4,5},{5,4},{6,7},{7,6},{8,9},{9,8},{10,11... | collective-permute-start | bytes 1572872 | tf_op jit(solution)/shard_map/ppermute | solution.py:451
